TPU v7x, 256 devices: a whole 4x4x8 slice. The times are simulated.
256 devices in a mesh: view: 8 (over x, z_hi), tile: 32 (over y, z_lo, core).
Axes of the slice: x: 4, y: 4, z: 8 (z_hi: 2, z_lo: 4; z = z_hi * 4 + z_lo), core: 2. Of those that a mesh axis runs over, the one named last changes fastest.
Arguments:
- estimate: float32 [512, 12288], P('tile'), may hold values from 0.5 to 2
- recorded: float32 [8, 512, 12288], P('view', 'tile'), may hold values from 0.5 to 4
- kernels: float32 [8, 31, 192], P('view'), may hold values from 0.01 to 0.06
- illuminated: int32 [8, 32], P('view', 'tile'), may hold values 0 or 1
- detection: int32 [8], P('view'), may hold values from 0 to 2, as said below
Outputs:
- deconvolved: float32 [512, 12288], P('tile')
Inputs may be any that keep to these rules, and one draw needn't show every extreme that they name: `detection`: each of 0, 1 and 2 is some view's value when there are three views or more; 0 is always some view's value.
All inputs are finite; a program needn't handle non-finite values. No bound on the sum of `illuminated` on one device may be relied on, other than what follows from the above.
Results may differ from a plain program's by a relative error of at most 0.0003.
Values sent between devices are 32-bit elements; how exact they have to be, the bound alone decides.
A program may use at most 128 MiB of HBM per device.

v0:
```python
import jax
import jax.numpy as jnp
from jax import lax
from jax.sharding import PartitionSpec as P

YW = 64
Z = 192
ITERS = 2


def extended_2(cells, sides, width):
    for axis, dim in sides:
        count = lax.axis_size(axis)
        ends = count - 1
        head = lax.slice_in_dim(cells, 0, width, axis=dim)
        tail = lax.slice_in_dim(cells, cells.shape[dim] - width, cells.shape[dim], axis=dim)
        cells = jnp.concatenate(
            [
                lax.ppermute(tail, axis, [(i, (i + 1) % count) for i in range(ends)]),
                cells,
                lax.ppermute(head, axis, [((i + 1) % count, i) for i in range(ends)]),
            ],
            axis=dim,
        )
    return cells


def tap_rows(taps):
    return jnp.tile(taps, (1, YW))


def depth_valid(shift_by):
    depth = jnp.arange(YW * Z, dtype=jnp.int32) % Z
    moved = depth + shift_by
    return ((moved >= 0) & (moved < Z)).astype(jnp.float32)


def pad_columns(flat, width):
    return jnp.pad(flat, ((0, 0), (width, width)))


def forward_first(extended, volume, taps):
    radius = taps.shape[0] // 2
    coefs = tap_rows(taps)
    planes = volume.shape[0]
    result = jnp.zeros(volume.shape, jnp.float32)
    for offset in range(2 * radius + 1):
        result = result + coefs[offset] * lax.slice_in_dim(
            extended, offset, offset + planes, axis=0
        )
    return result


def forward_second(extended, volume, taps):
    radius = taps.shape[0] // 2
    coefs = tap_rows(taps)
    length = volume.shape[1]
    padded = pad_columns(volume, radius * Z)
    result = jnp.zeros(volume.shape, jnp.float32)
    for offset in range(2 * radius + 1):
        begin = offset * Z
        result = result + coefs[offset] * lax.slice_in_dim(padded, begin, begin + length, axis=1)
    return result


def forward_depth(extended, volume, taps):
    radius = taps.shape[0] // 2
    coefs = tap_rows(taps)
    length = volume.shape[1]
    padded = pad_columns(volume, radius)
    result = jnp.zeros(volume.shape, jnp.float32)
    for offset in range(2 * radius + 1):
        weight_row = coefs[offset] * depth_valid(offset - radius)
        result = result + weight_row * lax.slice_in_dim(padded, offset, offset + length, axis=1)
    return result


def adjoint_first(extended, ratio, taps):
    radius = taps.shape[0] // 2
    coefs = tap_rows(taps)
    planes = ratio.shape[0]
    result = jnp.zeros(ratio.shape, jnp.float32)
    for offset in range(2 * radius + 1):
        begin = 2 * radius - offset
        result = result + coefs[offset] * lax.slice_in_dim(extended, begin, begin + planes, axis=0)
    return result


def adjoint_second(extended, ratio, taps):
    radius = taps.shape[0] // 2
    coefs = tap_rows(taps)
    length = ratio.shape[1]
    padded = pad_columns(ratio, radius * Z)
    result = jnp.zeros(ratio.shape, jnp.float32)
    for offset in range(2 * radius + 1):
        begin = (2 * radius - offset) * Z
        result = result + coefs[offset] * lax.slice_in_dim(padded, begin, begin + length, axis=1)
    return result


def adjoint_depth(extended, ratio, taps):
    radius = taps.shape[0] // 2
    coefs = tap_rows(taps)
    length = ratio.shape[1]
    result = jnp.zeros(ratio.shape, jnp.float32)
    for offset in range(2 * radius + 1):
        padded = pad_columns(coefs[offset] * ratio, radius)
        begin = 2 * radius - offset
        result = result + depth_valid(radius - offset) * lax.slice_in_dim(
            padded, begin, begin + length, axis=1
        )
    return result


def estimate_with_rim(volume, radius):
    return extended_2(volume, (("tile", 0),), radius)


def on_device(estimate, recorded, kernels, illuminated, detection):
    taps = kernels[0]
    measured = recorded[0]
    detect_axis = detection[0]
    tile_lit = illuminated[0, 0] > 0
    view_count = lax.axis_size("view")
    radius = taps.shape[0] // 2
    forwards = [forward_first, forward_second, forward_depth]
    adjoints = [adjoint_first, adjoint_second, adjoint_depth]
    volume = estimate
    extended = estimate_with_rim(volume, radius)
    for iteration in range(ITERS):
        blurred = lax.switch(detect_axis, forwards, extended, volume, taps)
        ratio = measured / blurred
        ratio_wide = extended_2(ratio, (("tile", 0),), radius)
        factor = jnp.where(
            tile_lit, lax.switch(detect_axis, adjoints, ratio_wide, ratio, taps), 1.0
        )
        summed_all = lax.psum(factor, "view")
        volume = volume * summed_all / view_count
        if iteration + 1 < ITERS:
            extended = estimate_with_rim(volume, radius)
    return volume


def solution(mesh):
    in_specs = (
        P("tile", None),
        P("view", "tile", None),
        P("view", None, None),
        P("view", "tile"),
        P("view"),
    )
    out_specs = P("tile", None)
    return jax.shard_map(
        on_device, mesh=mesh, in_specs=in_specs, out_specs=out_specs, check_vma=False
    )
```

profile of v0, /device:TPU:4, one launch (start us, length us, event | category | flops | bytes accessed | tf_op | source)
XLA Modules:
  0.0 513.0 jit_solution(3515160599654868636)
XLA Ops:
  6.5 1.5 fusion.1049
  8.1 1.8 collective-permute-start
  9.9 1.3 collective-permute-start.1
  11.9 3.9 collective-permute-done.1
  16.0 42.0 %conditional.4 = (f32[16,12288]{1,0:T(8,128)}) conditional(s32[]{:T(128)} %bitcast.373, (f32[1,31,192]{2,0,1:T(1,128)S(1)}, f32[46,12288]{1,0:T(8,128)S(1)}, f32[16,12288]{1,0:T(8,128)S(1)}) %tuple.548, (f32[1,31,192]{2,0,1:T(1,128)S(1)}, f32[16,12288]{1,0:T(8,128)S(1)}) %tuple.549, (f32[1,31,192]{2,0,1:T(1,128)S(1)}, ...), branch_computations={%region_0.0_spmd, %region_1.2_spmd, %region_2.3_spmd} | conditional | flops 15065088 | bytes 31474980 | solution.py:131
  27.6 0.7 tile.161
  29.7 0.7 tile.165
  32.5 1.6 fusion.1023
  36.8 0.7 tile.129
  46.4 0.7 tile.59
  47.1 4.8 multiply_add_fusion
  58.0 1.5 bitcast_divide_fusion.1
  59.6 18.7 %collective-permute-start.2 = (f32[15,12288]{1,0:T(8,128)S(1)}, f32[15,12288]{1,0:T(8,128)S(1)}, u32[]{:S(2)}, u32[]{:S(2)}) collective-permute-start(f32[15,12288]{1,0:T(8,128)S(1)} %get-tuple-element.689), channel_id=1, source_target_pairs={{0,1},{1,2},{2,3},{3,4},{4,5},{5,6},{6,7},{7,8},{8,9},{9,10},{10,1... | collective-permute-start | bytes 2211848 | tf_op jit(solution)/shard_map/ppermute | solution.py:19
  78.3 1.3 collective-permute-start.3
  80.3 2.2 collective-permute-done.3
  82.8 42.3 %conditional.5 = (f32[16,12288]{1,0:T(8,128)}) conditional(s32[]{:T(128)} %bitcast.373, (f32[1,31,192]{2,0,1:T(1,128)S(1)}, f32[46,12288]{1,0:T(8,128)S(1)}, f32[16,12288]{1,0:T(8,128)S(1)}) %tuple.551, (f32[1,31,192]{2,0,1:T(1,128)S(1)}, f32[16,12288]{1,0:T(8,128)S(1)}) %tuple.552, (f32[1,31,192]{2,0,1:T(1,128)S(1)}, ...), branch_computations={%region_3.4_spmd, %region_4.5_spmd, %region_5.6_spmd} | conditional | flops 21159936 | bytes 59592968 | solution.py:135
  94.4 0.7 tile.531
  97.2 0.7 tile.537
  99.3 1.6 fusion.1029
  103.6 0.7 tile.427
  113.1 0.7 tile.543
  113.8 4.7 multiply_add_fusion.2
  125.1 2.1 broadcast_select_fusion.1
  127.3 137.6 %all-reduce.69.cloned.1.call-done = f32[16,12288]{1,0:T(8,128)} async-done(((f32[16,12288]{1,0:T(8,128)}), f32[16,12288]{1,0:T(8,128)}) %all-reduce.69.cloned.1.call-update) | async-done | bytes 786448 | tf_op jit(solution)/shard_map/psum | solution.py:137
  264.9 1.2 multiply_multiply_fusion.1
  266.2 1.3 collective-permute-start.4
  267.6 1.3 collective-permute-start.5
  269.4 2.3 collective-permute-done.5
  272.0 42.1 %conditional.6 = (f32[16,12288]{1,0:T(8,128)}) conditional(s32[]{:T(128)} %bitcast.373, (f32[1,31,192]{2,0,1:T(1,128)S(1)}, f32[46,12288]{1,0:T(8,128)S(1)}, f32[16,12288]{1,0:T(8,128)S(1)}) %tuple.554, (f32[1,31,192]{2,0,1:T(1,128)S(1)}, f32[16,12288]{1,0:T(8,128)S(1)}) %tuple.555, (f32[1,31,192]{2,0,1:T(1,128)S(1)}, ...), branch_computations={%region_7.8_spmd, %region_8.9_spmd, %region_9.10_spmd} | conditional | flops 15065088 | bytes 31474980 | solution.py:131
  279.5 0.7 tile.897
  288.5 1.6 fusion.1035
  295.5 0.7 tile.803
  303.2 4.8 multiply_add_fusion.3
  314.1 1.5 bitcast_divide_fusion
  315.7 14.4 %collective-permute-start.6 = (f32[15,12288]{1,0:T(8,128)S(1)}, f32[15,12288]{1,0:T(8,128)S(1)}, u32[]{:S(2)}, u32[]{:S(2)}) collective-permute-start(f32[15,12288]{1,0:T(8,128)S(1)} %get-tuple-element.685), channel_id=1, source_target_pairs={{0,1},{1,2},{2,3},{3,4},{4,5},{5,6},{6,7},{7,8},{8,9},{9,10},{10,1... | collective-permute-start | bytes 2211848 | tf_op jit(solution)/shard_map/ppermute | solution.py:19
  330.1 1.3 collective-permute-start.7
  331.9 2.3 collective-permute-done.7
  334.5 26.7 %conditional.7 = (f32[16,12288]{1,0:T(8,128)}) conditional(s32[]{:T(128)} %bitcast.373, (f32[1,31,192]{2,0,1:T(1,128)S(1)}, f32[46,12288]{1,0:T(8,128)S(1)}, f32[16,12288]{1,0:T(8,128)S(1)}) %tuple.557, (f32[1,31,192]{2,0,1:T(1,128)S(1)}, f32[16,12288]{1,0:T(8,128)S(1)}) %tuple.558, (f32[1,31,192]{2,0,1:T(1,128)S(1)}, ...), branch_computations={%region_10.11_spmd, %region_11.12_spmd, %region_12.13_spmd} | conditional | flops 21159936 | bytes 59592968 | solution.py:135
  337.9 0.7 tile.1265
  340.0 0.7 tile.1271
  345.7 1.0 fusion.1041
  349.5 0.7 tile.1175
  350.2 0.7 tile.1177
  353.0 0.7 tile.1247
  355.2 4.8 multiply_add_fusion.5
  361.2 2.2 broadcast_select_fusion
  363.4 140.0 %all-reduce.71.cloned.1.call-done = f32[16,12288]{1,0:T(8,128)} async-done(((f32[16,12288]{1,0:T(8,128)}), f32[16,12288]{1,0:T(8,128)}) %all-reduce.71.cloned.1.call-update) | async-done | bytes 786448 | tf_op jit(solution)/shard_map/psum | solution.py:137
  503.5 2.1 multiply_multiply_fusion
  (274 shorter events, 99.7 us)
Async XLA Ops:
  6.5 9.2 %copy-start.2 = (f32[16,12288]{1,0:T(8,128)S(1)}, f32[16,12288]{1,0:T(8,128)}, u32[]{:S(2)}) copy-start(f32[16,12288]{1,0:T(8,128)} %param.17) | copy-start | bytes 2359300
  6.5 258.3 %all-reduce.69.cloned.1.call-start = ((), (), s32[]{:S(2)}) async-start(), calls=%async_computation | async-start | bytes 1572864 | tf_op jit(solution)/shard_map/psum | solution.py:137
  8.1 3.8 collective-permute-start
  9.9 5.8 %collective-permute-start.1 = (f32[15,12288]{1,0:T(8,128)S(1)}, f32[15,12288]{1,0:T(8,128)S(1)}, u32[]{:S(2)}, u32[]{:S(2)}) collective-permute-start(f32[15,12288]{1,0:T(8,128)S(1)} %get-tuple-element.692), channel_id=1, source_target_pairs={{1,0},{2,1},{3,2},{4,3},{5,4},{6,5},{7,6},{8,7},{9,8},{10,9},{11,1... | collective-permute-start | bytes 2211848 | tf_op jit(solution)/shard_map/ppermute | solution.py:21
  11.8 4.1 copy-start.4
  16.0 0.6 copy-start.5
  59.6 20.6 %collective-permute-start.2 = (f32[15,12288]{1,0:T(8,128)S(1)}, f32[15,12288]{1,0:T(8,128)S(1)}, u32[]{:S(2)}, u32[]{:S(2)}) collective-permute-start(f32[15,12288]{1,0:T(8,128)S(1)} %get-tuple-element.689), channel_id=1, source_target_pairs={{0,1},{1,2},{2,3},{3,4},{4,5},{5,6},{6,7},{7,8},{8,9},{9,10},{10,1... | collective-permute-start | bytes 2211848 | tf_op jit(solution)/shard_map/ppermute | solution.py:19
  78.3 4.2 collective-permute-start.3
  82.8 0.6 copy-start.6
  125.1 139.8 %copy-start.3 = (f32[16,12288]{1,0:T(8,128)S(1)}, f32[16,12288]{1,0:T(8,128)}, u32[]{:S(2)}) copy-start(f32[16,12288]{1,0:T(8,128)} %param.17) | copy-start | bytes 2359300
  127.3 376.2 %all-reduce.71.cloned.1.call-start = ((), (), s32[]{:S(2)}) async-start(), calls=%async_computation.1 | async-start | bytes 1572864 | tf_op jit(solution)/shard_map/psum | solution.py:137
  266.1 5.9 %copy-start = (f32[16,12288]{1,0:T(8,128)}, f32[16,12288]{1,0:T(8,128)S(1)}, u32[]{:S(2)}) copy-start(f32[16,12288]{1,0:T(8,128)S(1)} %multiply_multiply_fusion.1) | copy-start | bytes 2359300
  266.2 3.2 collective-permute-start.4
  267.6 4.2 collective-permute-start.5
  272.0 0.6 copy-start.7
  315.7 16.2 %collective-permute-start.6 = (f32[15,12288]{1,0:T(8,128)S(1)}, f32[15,12288]{1,0:T(8,128)S(1)}, u32[]{:S(2)}, u32[]{:S(2)}) collective-permute-start(f32[15,12288]{1,0:T(8,128)S(1)} %get-tuple-element.685), channel_id=1, source_target_pairs={{0,1},{1,2},{2,3},{3,4},{4,5},{5,6},{6,7},{7,8},{8,9},{9,10},{10,1... | collective-permute-start | bytes 2211848 | tf_op jit(solution)/shard_map/ppermute | solution.py:19
  330.1 4.2 collective-permute-start.7
  334.5 0.6 copy-start.8
  361.2 142.3 %copy-start.1 = (f32[16,12288]{1,0:T(8,128)S(1)}, f32[16,12288]{1,0:T(8,128)}, u32[]{:S(2)}) copy-start(f32[16,12288]{1,0:T(8,128)} %copy-done) | copy-start | bytes 2359300
Sparse Core Ops, SparseCore 0:
  127.4 137.4 all-reduce.68
  363.5 139.8 all-reduce.70
where the time goes:
time: 521 us; the launch traced here: 513 us
  waiting for transfers between devices  289 us (55%)
  local copies, waits for them, and re-layouts  115 us (22%)
  starting transfers between devices  41.4 us (8%)
  other arithmetic  30.6 us (6%)
  loops' own time  20.7 us (4%)
  between operations  15.5 us (3%)
    psum x2, waiting for transfers between devices, on_device(): summed_all = lax.psum(factor, 'view')  278 us
    another operation x248, local copies, waits for them, and re-layouts, tap_rows(): return jnp.tile(taps, (1, YW))  105 us
    ppermute x4, starting transfers between devices, extended_2(): lax.ppermute(tail, axis, [(i, (i + 1) % count) for i in range(ends)])  36.2 us
    another operation x2, loops' own time, on_device(): blurred = lax.switch(detect_axis, forwards, extended, volume, taps)  12.6 us
    ppermute x4, waiting for transfers between devices, extended_2(): lax.ppermute(head, axis, [((i + 1) % count, i) for i in range(ends)])  10.8 us
  transfers between devices with their start and end apart: 10, of which 8 were waited for; matrix products, arithmetic and copies ran while one was open for 0% of the time, Pallas kernels for 0%

commit v1 on v0

v1 whole, which is shorter than its diff:
```python
import jax
import jax.numpy as jnp
from jax import lax
from jax.experimental import pallas as pl
from jax.experimental.pallas import tpu as pltpu
from jax.sharding import PartitionSpec as P


YW = 64
Z = 192
TAPS = 31
HALF = 15
ITERS = 2
VIEWS = 8
XC = 4
TILES = 32
CX = 16
ROWS = 16
DEPTH = 96
LANES = 128
RIM = 16
CHUNK = ROWS * Z
PACKED = 12
PIECES = 2
MESH = pl.DeviceIdType.MESH
F32 = jnp.float32
HIGH = lax.Precision.HIGHEST


def lane_of(shape):
    return lax.broadcasted_iota(jnp.int32, shape, len(shape) - 1)


def roll(a, shift):
    return pltpu.roll(a, shift, a.ndim - 1)


def pair_halves(t0, t1, t2):
    lane = lane_of(t0.shape)
    a0 = roll(t0, 16)
    a1 = jnp.where(lane < 48, roll(t0, 48), roll(t1, 48))
    b0 = jnp.where(lane < 80, roll(t1, 80), roll(t2, 80))
    b1 = roll(t2, 112)
    return (a0, b0), (a1, b1)


def halves_pair(a0, a1, b0, b1):
    lane = lane_of(a0.shape)
    a1r, b0r = roll(a1, 80), roll(b0, 48)
    t0 = jnp.where(lane < 96, roll(a0, 112), a1r)
    t1 = jnp.where(lane < 64, a1r, b0r)
    t2 = jnp.where(lane < 32, b0r, roll(b1, 16))
    return t0, t1, t2


def pack(rows):
    lane = lane_of(rows[0].shape)
    inner = (lane >= RIM) & (lane < RIM + DEPTH)
    return [jnp.where(inner, rows[i], roll(rows[3], 96 - 32 * i)) for i in range(3)]


def unpack(tiles):
    lane = lane_of(tiles[0].shape)
    r = [roll(tiles[i], 32 + 32 * i) for i in range(3)]
    return [tiles[0], tiles[1], tiles[2], jnp.where(lane < 48, r[0], jnp.where(lane < 80, r[1], r[2]))]


def swap(a):
    return jnp.swapaxes(a, 0, 1)


def pack_rim(a, shift):
    lane = lane_of((32, LANES))
    out = jnp.zeros((32, LANES), F32)
    for g in range(8):
        moved = roll(a[32 * g : 32 * g + 32], lax.rem(shift + 16 * g, 128))
        out = jnp.where((lane >= 16 * g) & (lane < 16 * g + 16), moved, out)
    return out


def unpack_rim(p, first):
    lane = lane_of((32, LANES))
    keep = (lane >= first) & (lane < first + 16)
    return jnp.concatenate(
        [jnp.where(keep, roll(p, lax.rem(first + 128 - 16 * g, 128)), 0.0) for g in range(8)], axis=0
    )


def kernel(
    est_hbm, rec_hbm, ker_ref, lit_ref, det_ref, out_ref,
    est, rec, kpad, send, got, tap_send, tap_got, meta_send, meta_got, lit_send, lit_got,
    weight, band, grid, depth_in, rec_in, blurred, total, land, rim_send, rim_land, gathered,
    in_sem, a_s, a_r, t_s, t_r, m_s, m_r, l_s, l_r, h_s, h_r, g_s, g_r, z_s, z_r, f_s, f_r,
):
    view = lax.axis_index("view")
    tile = lax.axis_index("tile")
    cx, zh = view // 2, lax.rem(view, 2)
    upper = zh == 1

    def at(dx, dz):
        return lax.rem(cx + dx, XC) * 2 + lax.rem(zh + dz, 2)

    others = [(0, 1), (1, 1), (3, 1), (2, 1), (1, 0), (3, 0), (2, 0)]

    to_device = [
        (view, lax.rem(tile + TILES - 1, TILES)),
        (view, lax.rem(tile + 1, TILES)),
        (lax.rem(view + VIEWS - 2, VIEWS), tile),
        (lax.rem(view + 2, VIEWS), tile),
        (view + 1 - 2 * zh, tile),
    ]
    goes = [tile > 0, tile < TILES - 1, cx > 0, cx < XC - 1, None]
    comes = [tile < TILES - 1, tile > 0, cx < XC - 1, cx > 0, None]

    def when(cond, f):
        if cond is None:
            f()
        else:
            pl.when(cond)(f)

    barrier = pltpu.get_barrier_semaphore()

    def greet(device):
        pl.semaphore_signal(barrier, inc=1, device_id=device, device_id_type=MESH)

    for d in (0, 1):
        when(goes[d], lambda d=d: greet(to_device[d]))
    for dx, dz in others:
        greet((at(dx, dz), tile))

    est_in = pltpu.make_async_copy(est_hbm, est.at[:, pl.ds(CHUNK, YW * Z)], in_sem.at[0])
    rec_copy = pltpu.make_async_copy(rec_hbm.at[0], rec, in_sem.at[1])
    est_in.start()
    rec_copy.start()

    def rim_copy(phase, d, src, dst):
        return pltpu.make_async_remote_copy(
            src_ref=src, dst_ref=dst, send_sem=h_s.at[phase, d], recv_sem=h_r.at[phase, d],
            device_id=to_device[d], device_id_type=MESH,
        )

    def volume_rim(phase, d):
        if d == 4:
            return rim_copy(phase, d, rim_send.at[phase], rim_land.at[phase])
        layout = 1 if d < 2 else 0
        if d % 2 == 0:
            return rim_copy(phase, d, grid.at[layout, pl.ds(16, 15)], grid.at[layout, pl.ds(32, 15)])
        return rim_copy(phase, d, grid.at[layout, pl.ds(17, 15)], grid.at[layout, pl.ds(1, 15)])

    def sum_rim(phase, d):
        if d == 4:
            return rim_copy(phase, d, rim_send.at[phase], rim_land.at[phase])
        layout = 1 if d < 2 else 0
        first = 1 if d % 2 == 0 else 32
        return rim_copy(phase, d, total.at[layout, pl.ds(first, 15)], land.at[phase // 2, d])

    def start_rims(make, phase, dirs):
        for d in dirs:
            when(goes[d], lambda d=d: make(phase, d).start())

    def recv_rims(make, phase, dirs):
        for d in dirs:
            when(comes[d], lambda d=d: make(phase, d).wait_recv())

    def sent_rims(make, phase, dirs):
        for d in dirs:
            when(goes[d], lambda d=d: make(phase, d).wait_send())

    zero_rim = jnp.zeros((16, 16, LANES), F32)
    for d, into in ((0, 32), (1, 0)):
        @pl.when(jnp.logical_not(comes[d]))
        def _(d=d, into=into):
            grid[1, into : into + 16] = zero_rim
            lit_got[d] = jnp.zeros((8, LANES), F32)

    for d in range(4):
        @pl.when(jnp.logical_not(comes[d]))
        def _(d=d):
            for i in range(ITERS):
                land[i, d] = zero_rim[:15]

    lane32 = lane_of((32, LANES))
    inner32 = (lane32 >= RIM) & (lane32 < RIM + DEPTH)
    kpad[...] = jnp.zeros((32, 2 * LANES), F32)
    kpad[0:TAPS, 0:Z] = ker_ref[0]
    k0, k1 = kpad[:, 0:LANES], kpad[:, LANES : 2 * LANES]
    row8 = lax.broadcasted_iota(jnp.int32, (8, LANES), 0)
    axis_now = det_ref[0]
    flags = jnp.where(row8 == axis_now, 1.0, 0.0).astype(F32)
    tap_send[0, 0:32] = jnp.where(inner32, roll(k0, 16), 0.0)
    tap_send[1, 0:32] = jnp.where(inner32, jnp.where(lane32 < 48, roll(k0, 48), roll(k1, 48)), 0.0)
    tap_send[0, 32:40] = flags
    tap_send[1, 32:40] = flags
    tap_got[view] = tap_send[zh]
    lit_now = (lit_ref[0, 0] > 0).astype(F32)
    lit_send[...] = jnp.full((8, LANES), lit_now, F32)

    est[:, 0:CHUNK] = jnp.zeros((CX, CHUNK), F32)
    est[:, CHUNK + YW * Z : 2 * CHUNK + YW * Z] = jnp.zeros((CX, CHUNK), F32)
    est_in.wait()
    lane16 = lane_of((CX, LANES))
    edge = (lane16 >= jnp.where(upper, 0, RIM)) & (lane16 < jnp.where(upper, RIM + DEPTH, LANES))
    high_half = jnp.broadcast_to(zh, (CX, LANES)) == 1

    def est_pair(j, carry):
        base = pl.multiple_of(cx * CHUNK + j * 2 * Z, LANES)
        tiles = [est[:, pl.ds(base + LANES * i, LANES)] for i in range(3)]
        low, high = pair_halves(*tiles)
        for i in range(2):
            grid[0, 2 * j + i] = jnp.where(edge, jnp.where(high_half, high[i], low[i]), 0.0)
        return carry

    lax.fori_loop(0, 24, est_pair, 0)
    centre = grid[0, 16:32]
    depth_in[...] = centre
    grid[1, 16:32] = swap(centre)

    rec_copy.wait()

    def pack_rows(step, carry):
        rows, part = step // 4, lax.rem(step, 4)
        rows = lax.rem(cx + rows, XC)
        base = pl.multiple_of(rows * CHUNK + part * 4 * Z, LANES)
        tiles = [rec[:, pl.ds(base + LANES * i, LANES)] for i in range(6)]
        one, two = pair_halves(*tiles[:3]), pair_halves(*tiles[3:])
        for half in range(2):
            packed = pack([*one[half], *two[half]])
            for i in range(3):
                send[rows * 2 + half, part * 3 + i] = packed[i]
        return carry

    lax.fori_loop(0, 16, pack_rows, 0)
    got[view] = send[view]

    pl.semaphore_wait(barrier, 7 + (tile > 0).astype(jnp.int32) + (tile < TILES - 1).astype(jnp.int32))

    def to_view(v, src, dst, s, r):
        return pltpu.make_async_remote_copy(
            src_ref=src, dst_ref=dst, send_sem=s.at[v], recv_sem=r.at[v], device_id=(v, tile), device_id_type=MESH
        )

    def lit_copy(d):
        return pltpu.make_async_remote_copy(
            src_ref=lit_send, dst_ref=lit_got.at[d], send_sem=l_s.at[d], recv_sem=l_r.at[d],
            device_id=to_device[d], device_id_type=MESH,
        )

    def out_to(v, src, dst, s, r):
        return pltpu.make_async_remote_copy(
            src_ref=src, dst_ref=dst, send_sem=s.at[v], recv_sem=r.at[view], device_id=(v, tile), device_id_type=MESH
        )

    for d in (0, 1):
        when(goes[d], lambda d=d: lit_copy(d).start())
    for dx, dz in others:
        v = at(dx, dz)
        out_to(v, tap_send.at[lax.rem(v, 2)], tap_got.at[view], t_s, t_r).start()
    start_rims(volume_rim, 0, (0, 1))
    for dx, dz in others:
        v = at(dx, dz)
        out_to(v, send.at[v], got.at[view], a_s, a_r).start()

    for d in (0, 1):
        when(comes[d], lambda d=d: lit_copy(d).wait_recv())
    meta_send[...] = jnp.where(row8 == 0, lit_now, jnp.where(row8 == 1, lit_got[1], lit_got[0]))
    meta_got[view] = meta_send[...]
    for dx, dz in others:
        out_to(at(dx, dz), meta_send, meta_got.at[view], m_s, m_r).start()

    for dx, dz in others:
        v = at(dx, dz)
        to_view(v, tap_send.at[0], tap_got.at[v], t_s, t_r).wait_recv()

    def prepare(v, carry):
        taps = tap_got[v, 0:32]
        along_x = tap_got[v, 32:33]
        along_y = tap_got[v, 33:34]
        along_z = tap_got[v, 34:35]
        weight[v] = taps * (along_x + along_y)
        deep = jnp.concatenate([taps * along_z, jnp.zeros((LANES - 32, LANES), F32)], axis=0)
        band[v] = pltpu.roll(jnp.transpose(deep), LANES - HALF, 1, stride=1, stride_axis=0)
        return carry

    lax.fori_loop(0, VIEWS, prepare, 0)

    def blur_view(v, carry):
        first_dim = jnp.broadcast_to(tap_got[v, 32:33], (8, LANES)) > 0.5
        deep = lax.dot_general(
            depth_in[...].reshape(256, LANES), band[v], (((1,), (1,)), ((), ())),
            precision=HIGH, preferred_element_type=F32,
        ).reshape(16, 16, LANES)
        for s in range(2):
            for h in range(2):
                window = jnp.where(
                    first_dim[None],
                    grid[1, 8 * h + 1 : 8 * h + 39, 8 * s : 8 * s + 8],
                    grid[0, 8 * h + 1 : 8 * h + 39, 8 * s : 8 * s + 8],
                )
                acc = deep[8 * h : 8 * h + 8, 8 * s : 8 * s + 8]
                for k in range(TAPS):
                    acc = acc + window[k : k + 8] * weight[v, k : k + 1][None]
                blurred[v, 8 * h : 8 * h + 8, 8 * s : 8 * s + 8] = acc
        return carry

    lane3 = lane_of((16, 16, LANES))
    inner3 = (lane3 >= RIM) & (lane3 < RIM + DEPTH)

    def spread_view(v):
        along_x = jnp.broadcast_to(tap_got[v, 32:33], (8, LANES))
        along_y = jnp.broadcast_to(tap_got[v, 33:34], (8, LANES))
        lit = [jnp.broadcast_to(meta_got[v, i : i + 1], (8, LANES)) for i in range(3)]
        first_dim = along_x > 0.5
        ratio = jnp.where(
            inner3, jnp.where(jnp.broadcast_to(first_dim[:1][None], (16, 16, LANES)), rec_in[1, v], rec_in[0, v]) / blurred[v], 0.0
        )
        deep = lax.dot_general(
            ratio.reshape(256, LANES), band[v], (((1,), (0,)), ((), ())), precision=HIGH, preferred_element_type=F32
        ).reshape(16, 16, LANES)
        own = lit[0][:1][None]
        total[0, 16:32] += deep * own
        for s in range(2):
            r = ratio[:, 8 * s : 8 * s + 8]
            for block in range(3):
                first = (-HALF, 0, 16)[block]
                count = (HALF, 16, HALF)[block]
                acc = jnp.zeros((count, 8, LANES), F32)
                for k in range(TAPS):
                    lo = max(first, k - HALF)
                    hi = min(first + count, 16 + k - HALF)
                    if lo >= hi:
                        continue
                    part = r[lo - k + HALF : hi - k + HALF] * weight[v, k : k + 1][None]
                    pieces = []
                    if lo > first:
                        pieces.append(acc[: lo - first])
                    pieces.append(acc[lo - first : hi - first] + part)
                    if hi < first + count:
                        pieces.append(acc[hi - first :])
                    acc = jnp.concatenate(pieces, axis=0) if len(pieces) > 1 else pieces[0]
                where = slice(first + 16, first + 16 + count)
                lit_x = (lit[1], lit[0], lit[2])[block]
                total[1, where, 8 * s : 8 * s + 8] += acc * (along_x * lit_x)[None]
                total[0, where, 8 * s : 8 * s + 8] += acc * (along_y * lit[0])[None]

    def update(phase):
        for d in range(4):
            layout = 1 if d < 2 else 0
            first = 17 if d % 2 == 0 else 16
            total[layout, first : first + 15] += land[phase // 2, d]
        unlit = jnp.zeros((1, LANES), F32)
        for v in range(VIEWS):
            unlit = unlit + (1.0 - meta_got[v, 0:1])
        rim = unpack_rim(rim_land[phase], jnp.where(upper, 16, 96)).reshape(16, 16, LANES)
        summed = total[0, 16:32] + swap(total[1, 16:32]) + rim + unlit[None]
        return jnp.where(inner3, grid[0, 16:32] * summed * (1.0 / VIEWS), 0.0)

    recv_rims(volume_rim, 0, (0, 1))
    lax.fori_loop(0, VIEWS, blur_view, 0)

    def arrive(v):
        for part in range(4):
            rows = unpack([got[v, 3 * part + i] for i in range(3)])
            for i in range(4):
                rec_in[0, v, 4 * part + i] = rows[i]
        rec_in[1, v] = swap(rec_in[0, v])

    for dx, dz in others:
        v = at(dx, dz)
        to_view(v, meta_send, meta_got.at[v], m_s, m_r).wait_recv()

    total[...] = jnp.zeros((2, 48, 16, LANES), F32)
    arrive(view)
    spread_view(view)

    def spread_arrived(step, carry):
        order = lax.rem(step, 4)
        v = lax.rem(cx + order, XC) * 2 + lax.rem(zh + step // 4, 2)
        to_view(v, send.at[v], got.at[v], a_s, a_r).wait_recv()
        arrive(v)
        spread_view(v)
        return carry

    lax.fori_loop(1, VIEWS, spread_arrived, 0)

    def send_sums(phase):
        rim_send[phase] = pack_rim(total[0, 16:32].reshape(256, LANES), jnp.where(upper, 0, 16))
        start_rims(sum_rim, phase, range(5))

    sent_rims(volume_rim, 0, (0, 1))
    send_sums(1)
    recv_rims(sum_rim, 1, range(5))
    sent_rims(sum_rim, 1, range(5))
    fresh = update(1)
    grid[0, 16:32] = fresh
    start_rims(volume_rim, 2, (2, 3))
    grid[1, 16:32] = swap(fresh)
    start_rims(volume_rim, 2, (0, 1))
    rim_send[2] = pack_rim(fresh.reshape(256, LANES), jnp.where(upper, 112, 32))
    start_rims(volume_rim, 2, (4,))
    total[...] = jnp.zeros((2, 48, 16, LANES), F32)
    recv_rims(volume_rim, 2, range(5))
    depth_in[...] = grid[0, 16:32] + unpack_rim(rim_land[2], jnp.where(upper, 0, 112)).reshape(16, 16, LANES)

    def second(v, carry):
        blur_view(v, 0)
        spread_view(v)
        return carry

    lax.fori_loop(0, VIEWS, second, 0)
    send_sums(3)
    recv_rims(sum_rim, 3, range(5))
    fresh = update(3)

    for part in range(4):
        packed = pack([fresh[4 * part + i] for i in range(4)])
        for i in range(3):
            gathered[view, 3 * part + i] = packed[i]
    mate = at(0, 1)
    size = PACKED // PIECES

    def half_copy(i, block):
        cells = gathered.at[block, pl.ds(size * i, size)]
        return pltpu.make_async_remote_copy(
            src_ref=cells, dst_ref=cells, send_sem=z_s.at[i], recv_sem=z_r.at[i], device_id=(mate, tile), device_id_type=MESH
        )

    def row_copy(dx, block):
        cells = gathered.at[block]
        return pltpu.make_async_remote_copy(
            src_ref=cells, dst_ref=cells, send_sem=g_s.at[dx - 1], recv_sem=g_r.at[dx - 1],
            device_id=(at(dx, 0), tile), device_id_type=MESH,
        )

    def forward_copy(dx, i, block):
        cells = gathered.at[block, pl.ds(size * i, size)]
        return pltpu.make_async_remote_copy(
            src_ref=cells, dst_ref=cells, send_sem=f_s.at[dx - 1, i], recv_sem=f_r.at[dx - 1, i],
            device_id=(at(dx, 0), tile), device_id_type=MESH,
        )

    for i in range(PIECES):
        half_copy(i, view).start()
    for dx in (1, 3, 2):
        row_copy(dx, view).start()
    for i in range(PIECES):
        half_copy(i, mate).wait_recv()
        for dx in (1, 3, 2):
            forward_copy(dx, i, mate).start()

    def unpack_out(rows):
        for part in range(4):
            low = unpack([gathered[2 * rows, 3 * part + i] for i in range(3)])
            high = unpack([gathered[2 * rows + 1, 3 * part + i] for i in range(3)])
            base = pl.multiple_of(rows * CHUNK + part * 4 * Z, LANES)
            for p in range(2):
                for i, t in enumerate(halves_pair(low[2 * p], high[2 * p], low[2 * p + 1], high[2 * p + 1])):
                    out_ref[:, pl.ds(base + LANES * (3 * p + i), LANES)] = t

    unpack_out(cx)
    for dx in (1, 3, 2):
        source = at(XC - dx, 0)
        row_copy(dx, source).wait_recv()
        for i in range(PIECES):
            forward_copy(dx, i, at(XC - dx, 1)).wait_recv()
        unpack_out(source // 2)

    for d in (0, 1):
        when(goes[d], lambda d=d: lit_copy(d).wait_send())
    for dx, dz in others:
        v = at(dx, dz)
        out_to(v, tap_send.at[0], tap_got.at[view], t_s, t_r).wait_send()
        out_to(v, meta_send, meta_got.at[view], m_s, m_r).wait_send()
        out_to(v, send.at[v], got.at[view], a_s, a_r).wait_send()
    sent_rims(volume_rim, 2, range(5))
    sent_rims(sum_rim, 3, range(5))
    for i in range(PIECES):
        half_copy(i, view).wait_send()
    for dx in (1, 3, 2):
        row_copy(dx, view).wait_send()
        for i in range(PIECES):
            forward_copy(dx, i, mate).wait_send()


def on_device(estimate, recorded, kernels, illuminated, detection):
    dma = pltpu.SemaphoreType.DMA
    vmem = lambda *shape: pltpu.VMEM(shape, F32)
    return pl.pallas_call(
        kernel,
        out_shape=jax.ShapeDtypeStruct((CX, YW * Z), F32),
        in_specs=[
            pl.BlockSpec(memory_space=pl.ANY),
            pl.BlockSpec(memory_space=pl.ANY),
            pl.BlockSpec(memory_space=pltpu.VMEM),
            pl.BlockSpec(memory_space=pltpu.SMEM),
            pl.BlockSpec(memory_space=pltpu.SMEM),
        ],
        out_specs=pl.BlockSpec(memory_space=pltpu.VMEM),
        scratch_shapes=[
            vmem(CX, YW * Z + 2 * CHUNK),
            vmem(CX, YW * Z),
            vmem(32, 2 * LANES),
            vmem(VIEWS, PACKED, CX, LANES),
            vmem(VIEWS, PACKED, CX, LANES),
            vmem(2, 40, LANES),
            vmem(VIEWS, 40, LANES),
            vmem(8, LANES),
            vmem(VIEWS, 8, LANES),
            vmem(8, LANES),
            vmem(2, 8, LANES),
            vmem(VIEWS, 32, LANES),
            vmem(VIEWS, LANES, LANES),
            vmem(2, 48, 16, LANES),
            vmem(16, 16, LANES),
            vmem(2, VIEWS, 16, 16, LANES),
            vmem(VIEWS, 16, 16, LANES),
            vmem(2, 48, 16, LANES),
            vmem(ITERS, 4, HALF, 16, LANES),
            vmem(4, 32, LANES),
            vmem(4, 32, LANES),
            vmem(VIEWS, PACKED, CX, LANES),
            dma((2,)),
            dma((VIEWS,)), dma((VIEWS,)),
            dma((VIEWS,)), dma((VIEWS,)),
            dma((VIEWS,)), dma((VIEWS,)),
            dma((2,)), dma((2,)),
            dma((4, 5)), dma((4, 5)),
            dma((3,)), dma((3,)),
            dma((PIECES,)), dma((PIECES,)),
            dma((3, PIECES)), dma((3, PIECES)),
        ],
        compiler_params=pltpu.CompilerParams(
            collective_id=0, has_side_effects=True, vmem_limit_bytes=40 * 1024 * 1024
        ),
    )(estimate, recorded, kernels, illuminated, detection)


def solution(mesh):
    in_specs = (
        P("tile", None),
        P("view", "tile", None),
        P("view", None, None),
        P("view", "tile"),
        P("view"),
    )
    return jax.shard_map(
        on_device, mesh=mesh, in_specs=in_specs, out_specs=P("tile", None), check_vma=False
    )
```

time: 521 us -> 90 us (0.17)
  the two profiles are of different devices: /device:TPU:4 before, /device:TPU:32 now
where the time goes in v1:
time: 90 us; the launch traced here: 89.3 us
  Pallas kernels  84.1 us (93%)
  local copies, waits for them, and re-layouts  3.91 us (4%)
  between operations  1.31 us (1%)
    pallas_call x1, Pallas kernels, on_device(): pl.pallas_call(kernel, out_shape=jax.ShapeDtypeStruct((CX, YW * Z), F32),...  84.1 us
    unnamed x6, local copies, waits for them, and re-layouts  3.91 us

profile of v1, /device:TPU:32, one launch (start us, length us, event | category | flops | bytes accessed | tf_op | source)
XLA Modules:
  0.0 89.3 jit_solution(10435636969603767204)
XLA Ops:
  1.3 0.8 copy.6.ker_ref
  2.1 0.0 copy-start
  2.1 1.1 %copy-done = f32[16,12288]{1,0:T(8,128)S(1)} copy-done((f32[16,12288]{1,0:T(8,128)S(1)}, f32[16,12288]{1,0:T(8,128)}, u32[]{:S(2)}) %copy-start) | copy-done | bytes 786456
  3.2 0.0 copy-start.1
  3.2 1.1 %copy-done.1 = f32[1,16,12288]{2,1,0:T(8,128)S(1)} copy-done((f32[1,16,12288]{2,1,0:T(8,128)S(1)}, f32[1,16,12288]{2,1,0:T(8,128)}, u32[]{:S(2)}) %copy-start.1) | copy-done | bytes 786456
  4.3 84.1 %shard_map.55 = f32[16,12288]{1,0:T(8,128)S(1)} custom-call(f32[16,12288]{1,0:T(8,128)S(1)} %copy-done, f32[1,16,12288]{2,1,0:T(8,128)S(1)} %copy-done.1, f32[1,31,192]{2,1,0:T(8,128)S(1)} %copy.6.ker_ref, s32[1,1]{1,0:T(1,128)S(6)} %copy.8.lit_ref, s32[1]{0:T(128)S(6)} %copy.9.det_ref), custom_call_target="tpu_custom_call" | custom-call | tf_op jit(solution)/shard_map/pallas_call | solution.py:487
  88.4 0.9 copy.10
Async XLA Ops:
  2.1 1.1 %copy-start = (f32[16,12288]{1,0:T(8,128)S(1)}, f32[16,12288]{1,0:T(8,128)}, u32[]{:S(2)}) copy-start(f32[16,12288]{1,0:T(8,128)} %est_hbm.1) | copy-start | bytes 2359300
  3.2 1.1 %copy-start.1 = (f32[1,16,12288]{2,1,0:T(8,128)S(1)}, f32[1,16,12288]{2,1,0:T(8,128)}, u32[]{:S(2)}) copy-start(f32[1,16,12288]{2,1,0:T(8,128)} %rec_hbm.1) | copy-start | bytes 2359300

commit v2 on v1

v2 whole, which is shorter than its diff:
```python
import jax
import jax.numpy as jnp
from jax import lax
from jax.experimental import pallas as pl
from jax.experimental.pallas import tpu as pltpu
from jax.sharding import PartitionSpec as P


YW = 64
Z = 192
TAPS = 31
HALF = 15
ITERS = 2
VIEWS = 8
XC = 4
TILES = 32
CX = 16
ROWS = 16
DEPTH = 96
LANES = 128
RIM = 16
CHUNK = ROWS * Z
PACKED = 12
PIECES = 4
VMEM_BYTES = 60 * 1024 * 1024
MESH = pl.DeviceIdType.MESH
F32 = jnp.float32
BF16 = jnp.bfloat16


def lane_of(shape):
    return lax.broadcasted_iota(jnp.int32, shape, len(shape) - 1)


def roll(a, shift):
    return pltpu.roll(a, shift, a.ndim - 1)


def pair_halves(t0, t1, t2):
    lane = lane_of(t0.shape)
    a0 = roll(t0, 16)
    a1 = jnp.where(lane < 48, roll(t0, 48), roll(t1, 48))
    b0 = jnp.where(lane < 80, roll(t1, 80), roll(t2, 80))
    b1 = roll(t2, 112)
    return (a0, b0), (a1, b1)


def halves_pair(a0, a1, b0, b1):
    lane = lane_of(a0.shape)
    a1r, b0r = roll(a1, 80), roll(b0, 48)
    t0 = jnp.where(lane < 96, roll(a0, 112), a1r)
    t1 = jnp.where(lane < 64, a1r, b0r)
    t2 = jnp.where(lane < 32, b0r, roll(b1, 16))
    return t0, t1, t2


def pack(rows):
    lane = lane_of(rows[0].shape)
    inner = (lane >= RIM) & (lane < RIM + DEPTH)
    return [jnp.where(inner, rows[i], roll(rows[3], 96 - 32 * i)) for i in range(3)]


def unpack(tiles):
    lane = lane_of(tiles[0].shape)
    r = [roll(tiles[i], 32 + 32 * i) for i in range(3)]
    return [tiles[0], tiles[1], tiles[2], jnp.where(lane < 48, r[0], jnp.where(lane < 80, r[1], r[2]))]


def swap(a):
    return jnp.swapaxes(a, 0, 1)


def pack_rim(a, shift):
    lane = lane_of((32, LANES))
    out = jnp.zeros((32, LANES), F32)
    for g in range(8):
        moved = roll(a[32 * g : 32 * g + 32], lax.rem(shift + 16 * g, 128))
        out = jnp.where((lane >= 16 * g) & (lane < 16 * g + 16), moved, out)
    return out


def unpack_rim(p, first):
    lane = lane_of((32, LANES))
    keep = (lane >= first) & (lane < first + 16)
    return jnp.concatenate(
        [jnp.where(keep, roll(p, lax.rem(first + 128 - 16 * g, 128)), 0.0) for g in range(8)], axis=0
    )


def split3(a, order):
    high = a.astype(BF16)
    low = (a - high.astype(F32)).astype(BF16)
    return jnp.concatenate([(high, low)[i] for i in order], axis=-1)


def kernel(
    est_hbm, rec_hbm, ker_hbm, lit_ref, det_ref, out_hbm,
    est, rec, kpad, send, got, tap_send, tap_got, lit_send, lit_got, flags_of,
    weight, band, band_t, grid, depth_in, rec_in, blurred, total, land, rim_send, rim_land, gathered, out,
    in_sem, out_sem, a_s, a_r, t_s, t_r, l_s, l_r, h_s, h_r, g_s, g_r, z_s, z_r, f_s, f_r,
):
    view = lax.axis_index("view")
    tile = lax.axis_index("tile")
    cx, zh = view // 2, lax.rem(view, 2)
    odd = lax.rem(tile // 8, 2)
    deep_half = lax.rem(zh + odd, 2)
    upper = deep_half == 1

    def at(dx, dz):
        return lax.rem(cx + dx, XC) * 2 + lax.rem(zh + dz, 2)

    mate = at(0, 1)
    others = [(0, 1), (1, 1), (1, 0), (3, 1), (3, 0), (2, 1), (2, 0)]

    to_device = [
        (jnp.where(lax.rem(tile, 8) == 0, mate, view), lax.rem(tile + TILES - 1, TILES)),
        (jnp.where(lax.rem(tile, 8) == 7, mate, view), lax.rem(tile + 1, TILES)),
        (lax.rem(view + VIEWS - 2, VIEWS), tile),
        (lax.rem(view + 2, VIEWS), tile),
        (mate, tile),
    ]
    goes = [tile > 0, tile < TILES - 1, cx > 0, cx < XC - 1, None]
    comes = [tile < TILES - 1, tile > 0, cx < XC - 1, cx > 0, None]

    def when(cond, f):
        if cond is None:
            f()
        else:
            pl.when(cond)(f)

    barrier = pltpu.get_barrier_semaphore()

    def greet(device):
        pl.semaphore_signal(barrier, inc=1, device_id=device, device_id_type=MESH)

    for dx, dz in others:
        greet((at(dx, dz), tile))
    for d in (0, 1):
        when(goes[d], lambda d=d: greet(to_device[d]))

    ROUND = (0, 1, 3, 2)

    def rec_in_copy(i):
        cells = pl.ds(pl.multiple_of(lax.rem(cx + ROUND[i], XC) * CHUNK, LANES), CHUNK)
        return pltpu.make_async_copy(rec_hbm.at[0, :, cells], rec.at[:, cells], in_sem.at[i])

    ker_copy = pltpu.make_async_copy(ker_hbm.at[0], kpad.at[:, :], in_sem.at[4])
    est_copy = pltpu.make_async_copy(est_hbm, est.at[:, pl.ds(CHUNK, YW * Z)], in_sem.at[5])
    ker_copy.start()
    for i in range(4):
        rec_in_copy(i).start()
    est_copy.start()

    def rim_copy(phase, d, src, dst):
        return pltpu.make_async_remote_copy(
            src_ref=src, dst_ref=dst, send_sem=h_s.at[phase, d], recv_sem=h_r.at[phase, d],
            device_id=to_device[d], device_id_type=MESH,
        )

    def volume_rim(phase, d):
        if d == 4:
            return rim_copy(phase, d, rim_send.at[phase], rim_land.at[phase])
        layout = 1 if d < 2 else 0
        if d % 2 == 0:
            return rim_copy(phase, d, grid.at[layout, pl.ds(16, 15)], grid.at[layout, pl.ds(32, 15)])
        return rim_copy(phase, d, grid.at[layout, pl.ds(17, 15)], grid.at[layout, pl.ds(1, 15)])

    def sum_rim(phase, d):
        if d == 4:
            return rim_copy(phase, d, rim_send.at[phase], rim_land.at[phase])
        layout = 1 if d < 2 else 0
        first = 1 if d % 2 == 0 else 32
        return rim_copy(phase, d, total.at[layout, pl.ds(first, 15)], land.at[phase // 2, d])

    def start_rims(make, phase, dirs):
        for d in dirs:
            when(goes[d], lambda d=d: make(phase, d).start())

    def recv_rims(make, phase, dirs):
        for d in dirs:
            when(comes[d], lambda d=d: make(phase, d).wait_recv())

    def sent_rims(make, phase, dirs):
        for d in dirs:
            when(goes[d], lambda d=d: make(phase, d).wait_send())

    def from_view(v, dst, r):
        return pltpu.make_async_remote_copy(
            src_ref=dst, dst_ref=dst, send_sem=r.at[v], recv_sem=r.at[v], device_id=(v, tile), device_id_type=MESH
        )

    def out_to(v, src, dst, s, r):
        return pltpu.make_async_remote_copy(
            src_ref=src, dst_ref=dst, send_sem=s.at[v], recv_sem=r.at[view], device_id=(v, tile), device_id_type=MESH
        )

    def lit_copy(d):
        return pltpu.make_async_remote_copy(
            src_ref=lit_send, dst_ref=lit_got.at[d], send_sem=l_s.at[d], recv_sem=l_r.at[d],
            device_id=to_device[d], device_id_type=MESH,
        )

    ker_copy.wait()
    lane32 = lane_of((32, LANES))
    row32 = lax.broadcasted_iota(jnp.int32, (32, LANES), 0)
    axis_now = det_ref[0].astype(F32)
    lit_now = (lit_ref[0, 0] > 0).astype(F32)
    flags = jnp.where(lane32 < 48, axis_now, lit_now)
    k0 = jnp.concatenate([kpad[:, 0:LANES], jnp.zeros((1, LANES), F32)], axis=0)
    k1 = jnp.concatenate([kpad[:, LANES:Z], jnp.zeros((TAPS, 2 * LANES - Z), F32)], axis=1)
    k1 = jnp.concatenate([k1, jnp.zeros((1, LANES), F32)], axis=0)
    for half in range(2):
        taps = roll(k0, 16) if half == 0 else jnp.where(lane32 < 48, roll(k0, 48), roll(k1, 48))
        taps = jnp.where(row32 == TAPS, flags, taps)
        for i, t in enumerate(pack([taps[8 * j : 8 * j + 8] for j in range(4)])):
            tap_send[half, i] = t
    tap_got[view] = tap_send[deep_half]

    def pack_rows(i):
        rec_in_copy(i).wait()
        rows = lax.rem(cx + ROUND[i], XC)

        def pack_part(part, carry):
            base = pl.multiple_of(rows * CHUNK + part * 4 * Z, LANES)
            tiles = [rec[:, pl.ds(base + LANES * j, LANES)] for j in range(6)]
            one, two = pair_halves(*tiles[:3]), pair_halves(*tiles[3:])
            for half in range(2):
                packed = pack([*one[half], *two[half]])
                for j in range(3):
                    send[rows * 2 + lax.rem(half + odd, 2), part * 3 + j] = packed[j]
            return carry

        lax.fori_loop(0, 4, pack_part, 0)

    def send_block(dx, dz):
        v = at(dx, dz)
        out_to(v, send.at[v], got.at[view], a_s, a_r).start()

    pack_rows(0)
    pl.semaphore_wait(barrier, 7 + (tile > 0).astype(jnp.int32) + (tile < TILES - 1).astype(jnp.int32))
    for dx, dz in others:
        v = at(dx, dz)
        out_to(v, tap_send.at[lax.rem(v + odd, 2)], tap_got.at[view], t_s, t_r).start()
    send_block(0, 1)
    for i in range(1, 4):
        pack_rows(i)
        send_block(ROUND[i], 1)
        send_block(ROUND[i], 0)
    got[view] = send[view]

    zero_rim = jnp.zeros((16, 16, LANES), F32)
    for d, into in ((0, 32), (1, 0)):
        @pl.when(jnp.logical_not(comes[d]))
        def _(d=d, into=into):
            grid[1, into : into + 16] = zero_rim
            lit_got[d] = jnp.zeros((8, LANES), F32)

    for d in range(4):
        @pl.when(jnp.logical_not(comes[d]))
        def _(d=d):
            for i in range(ITERS):
                land[i, d] = zero_rim[:15]

    est[:, 0:CHUNK] = jnp.zeros((CX, CHUNK), F32)
    est[:, CHUNK + YW * Z : 2 * CHUNK + YW * Z] = jnp.zeros((CX, CHUNK), F32)
    est_copy.wait()
    lane16 = lane_of((CX, LANES))
    edge = (lane16 >= jnp.where(upper, 0, RIM)) & (lane16 < jnp.where(upper, RIM + DEPTH, LANES))
    high_half = jnp.broadcast_to(deep_half, (CX, LANES)) == 1

    def est_pair(j, carry):
        base = pl.multiple_of(cx * CHUNK + j * 2 * Z, LANES)
        tiles = [est[:, pl.ds(base + LANES * i, LANES)] for i in range(3)]
        low, high = pair_halves(*tiles)
        for i in range(2):
            grid[0, 2 * j + i] = jnp.where(edge, jnp.where(high_half, high[i], low[i]), 0.0)
        return carry

    lax.fori_loop(8, 16, est_pair, 0)
    centre = grid[0, 16:32]
    grid[1, 16:32] = swap(centre)
    start_rims(volume_rim, 0, (0, 1))
    depth_in[...] = split3(centre.reshape(256, LANES), (0, 0, 1))
    lax.fori_loop(0, 8, est_pair, 0)
    lax.fori_loop(16, 24, est_pair, 0)

    for dx, dz in others:
        v = at(dx, dz)
        from_view(v, tap_got.at[v], t_r).wait_recv()

    def prepare(v, carry):
        taps = jnp.concatenate(unpack([tap_got[v, i] for i in range(3)]), axis=0)
        marks = taps[31:32]
        lane = lane_of((1, LANES))
        axis = jnp.sum(jnp.where(lane == 32, marks, 0.0), axis=1, keepdims=True)
        lit = jnp.sum(jnp.where(lane == 64, marks, 0.0), axis=1, keepdims=True)
        inner = (lane32 >= RIM) & (lane32 < RIM + DEPTH) & (row32 < TAPS)
        taps = jnp.where(inner, taps, 0.0)
        along = [jnp.broadcast_to(jnp.where(axis == float(d), 1.0, 0.0), (1, LANES)) for d in range(3)]
        lit = jnp.broadcast_to(lit, (1, LANES))
        flags_of[v] = jnp.concatenate([along[0], along[1], lit, jnp.zeros((5, LANES), F32)], axis=0)
        lit_send[pl.ds(v, 1)] = lit
        weight[v] = taps * (along[0] + along[1])
        deep = jnp.concatenate([taps * along[2], jnp.zeros((LANES - 32, LANES), F32)], axis=0)
        full = pltpu.roll(jnp.transpose(deep), LANES - HALF, 1, stride=1, stride_axis=0)
        band[v] = split3(full, (0, 1, 0))
        band_t[v] = split3(jnp.transpose(full), (0, 1, 0))
        return carry

    lax.fori_loop(0, VIEWS, prepare, 0)
    for d in (0, 1):
        when(goes[d], lambda d=d: lit_copy(d).start())

    def dot3(a, parts):
        out = jnp.zeros((256, LANES), F32)
        for i in range(3):
            out += jnp.dot(
                a[:, LANES * i : LANES * (i + 1)], parts[:, LANES * i : LANES * (i + 1)], preferred_element_type=F32
            )
        return out.reshape(16, 16, LANES)

    def tap_sum(out, first, count, source, origin, sign, v):
        length = source.shape[0]
        for k in range(TAPS):
            shift = sign * (k - HALF)
            lo = max(first, origin - shift)
            hi = min(first + count, origin + length - shift)
            if lo >= hi:
                continue
            part = source[lo + shift - origin : hi + shift - origin] * weight[v, k : k + 1][None]
            pieces = []
            if lo > first:
                pieces.append(out[: lo - first])
            pieces.append(out[lo - first : hi - first] + part)
            if hi < first + count:
                pieces.append(out[hi - first :])
            out = jnp.concatenate(pieces, axis=0) if len(pieces) > 1 else pieces[0]
        return out

    def along_x(v):
        return jnp.broadcast_to(flags_of[v, 0:1], (8, LANES))

    def in_layout(v, first, count, s):
        return jnp.where(
            (along_x(v) > 0.5)[None],
            grid[1, first : first + count, 8 * s : 8 * s + 8],
            grid[0, first : first + count, 8 * s : 8 * s + 8],
        )

    def blur_inside(v, carry):
        for s in range(2):
            blurred[v, :, 8 * s : 8 * s + 8] = tap_sum(
                jnp.zeros((16, 8, LANES), F32), 0, 16, in_layout(v, 16, 16, s), 0, 1, v
            )
        return carry

    def blur_rims(v, carry):
        deep = dot3(depth_in[...], band_t[v])
        for s in range(2):
            acc = blurred[v, :, 8 * s : 8 * s + 8] + deep[:, 8 * s : 8 * s + 8]
            acc = tap_sum(acc, 0, 16, in_layout(v, 1, 15, s), -15, 1, v)
            blurred[v, :, 8 * s : 8 * s + 8] = tap_sum(acc, 0, 16, in_layout(v, 32, 15, s), 16, 1, v)
        return carry

    lane3 = lane_of((16, 16, LANES))
    inner3 = (lane3 >= RIM) & (lane3 < RIM + DEPTH)

    def spread_rims(v):
        first_dim = jnp.broadcast_to((along_x(v) > 0.5)[None, :1], (16, 16, LANES))
        ratio = jnp.where(inner3, jnp.where(first_dim, rec_in[1, v], rec_in[0, v]) / blurred[v], 0.0)
        blurred[v] = ratio
        x = along_x(v)
        y = jnp.broadcast_to(flags_of[v, 1:2], (8, LANES))
        lit = jnp.broadcast_to(flags_of[v, 2:3], (8, LANES))
        deep = dot3(split3(ratio.reshape(256, LANES), (0, 0, 1)), band[v])
        total[0, 16:32] += deep * lit[:1][None]
        for s in range(2):
            r = ratio[:, 8 * s : 8 * s + 8]
            for first, row in ((-HALF, 1), (16, 0)):
                acc = tap_sum(jnp.zeros((HALF, 8, LANES), F32), first, HALF, r, 0, -1, v)
                cells = slice(first + 16, first + 16 + HALF)
                lit_x = jnp.broadcast_to(lit_got[row, pl.ds(v, 1)], (8, LANES))
                total[1, cells, 8 * s : 8 * s + 8] += acc * (x * lit_x)[None]
                total[0, cells, 8 * s : 8 * s + 8] += acc * (y * lit)[None]

    def spread_inside(v, carry):
        x = along_x(v)
        y = jnp.broadcast_to(flags_of[v, 1:2], (8, LANES))
        lit = jnp.broadcast_to(flags_of[v, 2:3], (8, LANES))
        for s in range(2):
            acc = tap_sum(
                jnp.zeros((16, 8, LANES), F32), 0, 16, blurred[v, :, 8 * s : 8 * s + 8], 0, -1, v
            )
            total[1, 16:32, 8 * s : 8 * s + 8] += acc * (x * lit)[None]
            total[0, 16:32, 8 * s : 8 * s + 8] += acc * (y * lit)[None]
        return carry

    def update(phase):
        for d in range(4):
            layout = 1 if d < 2 else 0
            first = 17 if d % 2 == 0 else 16
            total[layout, first : first + 15] += land[phase // 2, d]
        unlit = jnp.zeros((1, LANES), F32)
        for v in range(VIEWS):
            unlit = unlit + (1.0 - flags_of[v, 2:3])
        rim = unpack_rim(rim_land[phase], jnp.where(upper, 16, 96)).reshape(16, 16, LANES)
        summed = total[0, 16:32] + swap(total[1, 16:32]) + rim + unlit[None]
        return jnp.where(inner3, grid[0, 16:32] * summed * (1.0 / VIEWS), 0.0)

    lax.fori_loop(0, VIEWS, blur_inside, 0)
    recv_rims(volume_rim, 0, (0, 1))
    lax.fori_loop(0, VIEWS, blur_rims, 0)
    for d in (0, 1):
        when(comes[d], lambda d=d: lit_copy(d).wait_recv())

    def arrive(v):
        for part in range(4):
            rows = unpack([got[v, 3 * part + i] for i in range(3)])
            for i in range(4):
                rec_in[0, v, 4 * part + i] = rows[i]
        rec_in[1, v] = swap(rec_in[0, v])

    total[...] = jnp.zeros((2, 48, 16, LANES), F32)
    arrive(view)
    spread_rims(view)

    def spread_arrived(step, carry):
        order = lax.rem(step, 4)
        v = lax.rem(cx + order, XC) * 2 + lax.rem(zh + step // 4, 2)
        from_view(v, got.at[v], a_r).wait_recv()
        arrive(v)
        spread_rims(v)
        return carry

    lax.fori_loop(1, VIEWS, spread_arrived, 0)

    def send_sums(phase):
        start_rims(sum_rim, phase, range(4))
        rim_send[phase] = pack_rim(total[0, 16:32].reshape(256, LANES), jnp.where(upper, 0, 16))
        start_rims(sum_rim, phase, (4,))
        lax.fori_loop(0, VIEWS, spread_inside, 0)
        recv_rims(sum_rim, phase, range(5))

    sent_rims(volume_rim, 0, (0, 1))
    send_sums(1)
    fresh = update(1)
    grid[0, 16:32] = fresh
    start_rims(volume_rim, 2, (2, 3))
    grid[1, 16:32] = swap(fresh)
    start_rims(volume_rim, 2, (0, 1))
    rim_send[2] = pack_rim(fresh.reshape(256, LANES), jnp.where(upper, 112, 32))
    start_rims(volume_rim, 2, (4,))
    sent_rims(sum_rim, 1, range(5))
    total[...] = jnp.zeros((2, 48, 16, LANES), F32)
    lax.fori_loop(0, VIEWS, blur_inside, 0)
    recv_rims(volume_rim, 2, range(5))
    deep_rim = unpack_rim(rim_land[2], jnp.where(upper, 0, 112))
    depth_in[...] = split3(grid[0, 16:32].reshape(256, LANES) + deep_rim, (0, 0, 1))

    def second(v, carry):
        blur_rims(v, 0)
        spread_rims(v)
        return carry

    lax.fori_loop(0, VIEWS, second, 0)
    send_sums(3)
    fresh = update(3)

    for part in range(4):
        packed = pack([fresh[4 * part + i] for i in range(4)])
        for i in range(3):
            gathered[view, 3 * part + i] = packed[i]
    size = PACKED // PIECES

    def half_copy(i, block):
        cells = gathered.at[block, pl.ds(size * i, size)]
        return pltpu.make_async_remote_copy(
            src_ref=cells, dst_ref=cells, send_sem=z_s.at[i], recv_sem=z_r.at[i], device_id=(mate, tile), device_id_type=MESH
        )

    def row_copy(dx, block):
        cells = gathered.at[block]
        return pltpu.make_async_remote_copy(
            src_ref=cells, dst_ref=cells, send_sem=g_s.at[dx - 1], recv_sem=g_r.at[dx - 1],
            device_id=(at(dx, 0), tile), device_id_type=MESH,
        )

    def forward_copy(dx, i, block):
        cells = gathered.at[block, pl.ds(size * i, size)]
        return pltpu.make_async_remote_copy(
            src_ref=cells, dst_ref=cells, send_sem=f_s.at[dx - 1, i], recv_sem=f_r.at[dx - 1, i],
            device_id=(at(dx, 0), tile), device_id_type=MESH,
        )

    for i in range(PIECES):
        half_copy(i, view).start()
    for dx in (1, 3, 2):
        row_copy(dx, view).start()
    for i in range(PIECES):
        half_copy(i, mate).wait_recv()
        for dx in (1, 3, 2):
            forward_copy(dx, i, mate).start()

    def out_copy(i, rows):
        cells = pl.ds(pl.multiple_of(rows * CHUNK, LANES), CHUNK)
        return pltpu.make_async_copy(out.at[:, cells], out_hbm.at[:, cells], out_sem.at[i])

    def unpack_out(i, rows):
        for part in range(4):
            low = unpack([gathered[2 * rows + odd, 3 * part + j] for j in range(3)])
            high = unpack([gathered[2 * rows + 1 - odd, 3 * part + j] for j in range(3)])
            base = pl.multiple_of(rows * CHUNK + part * 4 * Z, LANES)
            for p in range(2):
                for j, t in enumerate(halves_pair(low[2 * p], high[2 * p], low[2 * p + 1], high[2 * p + 1])):
                    out[:, pl.ds(base + LANES * (3 * p + j), LANES)] = t
        out_copy(i, rows).start()

    unpack_out(0, cx)
    for n, dx in enumerate((1, 3, 2)):
        source = at(XC - dx, 0)
        row_copy(dx, source).wait_recv()
        for i in range(PIECES):
            forward_copy(dx, i, at(XC - dx, 1)).wait_recv()
        unpack_out(n + 1, source // 2)

    for d in (0, 1):
        when(goes[d], lambda d=d: lit_copy(d).wait_send())
    for dx, dz in others:
        v = at(dx, dz)
        out_to(v, tap_send.at[0], tap_got.at[view], t_s, t_r).wait_send()
        out_to(v, send.at[v], got.at[view], a_s, a_r).wait_send()
    sent_rims(volume_rim, 2, range(5))
    sent_rims(sum_rim, 3, range(5))
    for i in range(PIECES):
        half_copy(i, view).wait_send()
    for dx in (1, 3, 2):
        row_copy(dx, view).wait_send()
        for i in range(PIECES):
            forward_copy(dx, i, mate).wait_send()
    for i in range(4):
        out_copy(i, cx).wait()


def on_device(estimate, recorded, kernels, illuminated, detection):
    dma = pltpu.SemaphoreType.DMA
    vmem = lambda *shape: pltpu.VMEM(shape, F32)
    any_space = pl.BlockSpec(memory_space=pl.ANY)
    return pl.pallas_call(
        kernel,
        out_shape=jax.ShapeDtypeStruct((CX, YW * Z), F32),
        in_specs=[
            any_space,
            any_space,
            any_space,
            pl.BlockSpec(memory_space=pltpu.SMEM),
            pl.BlockSpec(memory_space=pltpu.SMEM),
        ],
        out_specs=any_space,
        scratch_shapes=[
            vmem(CX, YW * Z + 2 * CHUNK),
            vmem(CX, YW * Z),
            vmem(TAPS, Z),
            vmem(VIEWS, PACKED, CX, LANES),
            vmem(VIEWS, PACKED, CX, LANES),
            vmem(2, 3, 8, LANES),
            vmem(VIEWS, 3, 8, LANES),
            vmem(8, LANES),
            vmem(2, 8, LANES),
            vmem(VIEWS, 8, LANES),
            vmem(VIEWS, 32, LANES),
            pltpu.VMEM((VIEWS, LANES, 3 * LANES), BF16),
            pltpu.VMEM((VIEWS, LANES, 3 * LANES), BF16),
            vmem(2, 48, 16, LANES),
            pltpu.VMEM((256, 3 * LANES), BF16),
            vmem(2, VIEWS, 16, 16, LANES),
            vmem(VIEWS, 16, 16, LANES),
            vmem(2, 48, 16, LANES),
            vmem(ITERS, 4, HALF, 16, LANES),
            vmem(4, 32, LANES),
            vmem(4, 32, LANES),
            vmem(VIEWS, PACKED, CX, LANES),
            vmem(CX, YW * Z),
            dma((6,)),
            dma((4,)),
            dma((VIEWS,)), dma((VIEWS,)),
            dma((VIEWS,)), dma((VIEWS,)),
            dma((2,)), dma((2,)),
            dma((4, 5)), dma((4, 5)),
            dma((3,)), dma((3,)),
            dma((PIECES,)), dma((PIECES,)),
            dma((3, PIECES)), dma((3, PIECES)),
        ],
        compiler_params=pltpu.CompilerParams(
            collective_id=0, has_side_effects=True, vmem_limit_bytes=VMEM_BYTES
        ),
    )(estimate, recorded, kernels, illuminated, detection)


def solution(mesh):
    in_specs = (
        P("tile", None),
        P("view", "tile", None),
        P("view", None, None),
        P("view", "tile"),
        P("view"),
    )
    return jax.shard_map(
        on_device, mesh=mesh, in_specs=in_specs, out_specs=P("tile", None), check_vma=False
    )
```

time: 90 us -> 77.7 us (0.86)
  Pallas kernels: 84.1 us -> 72.7 us
    pallas_call x1, Pallas kernels: 84.1 us -> 72.7 us  [on_device(): pl.pallas_call(kernel, out_shape=jax.ShapeDtypeStruct((CX, YW * Z), F32),...]
    unnamed x6 -> x2, local copies, waits for them, and re-layouts: 3.91 us -> 3.44 us
where the time goes in v2:
time: 77.7 us; the launch traced here: 77.4 us
  Pallas kernels  72.7 us (94%)
  local copies, waits for them, and re-layouts  3.44 us (4%)
  between operations  1.31 us (2%)
    pallas_call x1, Pallas kernels, on_device(): pl.pallas_call(kernel, out_shape=jax.ShapeDtypeStruct((CX, YW * Z), F32),...  72.7 us
    unnamed x2, local copies, waits for them, and re-layouts  3.44 us

profile of v2, /device:TPU:32, one launch (start us, length us, event | category | flops | bytes accessed | tf_op | source)
XLA Modules:
  0.0 77.4 jit_solution(614470633391225344)
XLA Ops:
  1.3 1.4 %copy.6.ker_hbm = f32[1,31,192]{2,1,0:T(8,128)} copy(f32[1,31,192]{2,0,1:T(1,128)} %param.7) | data formatting | bytes 47616 | tf_op args[2]
  2.7 72.7 %shard_map.55 = f32[16,12288]{1,0:T(8,128)} custom-call(f32[16,12288]{1,0:T(8,128)} %est_hbm.1, f32[1,16,12288]{2,1,0:T(8,128)} %rec_hbm.1, f32[1,31,192]{2,1,0:T(8,128)} %copy.6.ker_hbm, s32[1,1]{1,0:T(1,128)S(6)} %copy.8.lit_ref, s32[1]{0:T(128)S(6)} %copy.9.det_ref), custom_call_target="tpu_custom_call" | custom-call | tf_op jit(solution)/shard_map/pallas_call | solution.py:548
  75.3 2.1 %copy.10 = f32[16,12288]{1,0:T(8,128)} copy(f32[16,12288]{1,0:T(8,128)} %shard_map.55) | data formatting | bytes 1572864

commit v3 on v2

--- a/solution.py
+++ b/solution.py
@@ -22,7 +22,7 @@
 CHUNK = ROWS * Z
 PACKED = 12
 PIECES = 4
-VMEM_BYTES = 60 * 1024 * 1024
+VMEM_BYTES = 53 * 1024 * 1024
 MESH = pl.DeviceIdType.MESH
 F32 = jnp.float32
 BF16 = jnp.bfloat16
@@ -94,10 +94,10 @@
 
 
 def kernel(
-    est_hbm, rec_hbm, ker_hbm, lit_ref, det_ref, out_hbm,
+    est_hbm, rec_hbm, ker_hbm, lit_ref, det_ref, out,
     est, rec, kpad, send, got, tap_send, tap_got, lit_send, lit_got, flags_of,
-    weight, band, band_t, grid, depth_in, rec_in, blurred, total, land, rim_send, rim_land, gathered, out,
-    in_sem, out_sem, a_s, a_r, t_s, t_r, l_s, l_r, h_s, h_r, g_s, g_r, z_s, z_r, f_s, f_r,
+    weight, band, band_t, grid, depth_in, rec_in, blurred, total, land, rim_send, rim_land, gathered,
+    in_sem, a_s, a_r, t_s, t_r, l_s, l_r, h_s, h_r, g_s, g_r, z_s, z_r, f_s, f_r,
 ):
     view = lax.axis_index("view")
     tile = lax.axis_index("tile")
@@ -144,7 +144,7 @@
         cells = pl.ds(pl.multiple_of(lax.rem(cx + ROUND[i], XC) * CHUNK, LANES), CHUNK)
         return pltpu.make_async_copy(rec_hbm.at[0, :, cells], rec.at[:, cells], in_sem.at[i])
 
-    ker_copy = pltpu.make_async_copy(ker_hbm.at[0], kpad.at[:, :], in_sem.at[4])
+    ker_copy = pltpu.make_async_copy(ker_hbm, kpad, in_sem.at[4])
     est_copy = pltpu.make_async_copy(est_hbm, est.at[:, pl.ds(CHUNK, YW * Z)], in_sem.at[5])
     ker_copy.start()
     for i in range(4):
@@ -206,8 +206,8 @@
     axis_now = det_ref[0].astype(F32)
     lit_now = (lit_ref[0, 0] > 0).astype(F32)
     flags = jnp.where(lane32 < 48, axis_now, lit_now)
-    k0 = jnp.concatenate([kpad[:, 0:LANES], jnp.zeros((1, LANES), F32)], axis=0)
-    k1 = jnp.concatenate([kpad[:, LANES:Z], jnp.zeros((TAPS, 2 * LANES - Z), F32)], axis=1)
+    k0 = jnp.concatenate([kpad[:, 0, 0:LANES], jnp.zeros((1, LANES), F32)], axis=0)
+    k1 = jnp.concatenate([kpad[:, 0, LANES:Z], jnp.zeros((TAPS, 2 * LANES - Z), F32)], axis=1)
     k1 = jnp.concatenate([k1, jnp.zeros((1, LANES), F32)], axis=0)
     for half in range(2):
         taps = roll(k0, 16) if half == 0 else jnp.where(lane32 < 48, roll(k0, 48), roll(k1, 48))
@@ -242,9 +242,11 @@
         v = at(dx, dz)
         out_to(v, tap_send.at[lax.rem(v + odd, 2)], tap_got.at[view], t_s, t_r).start()
     send_block(0, 1)
-    for i in range(1, 4):
+    pack_rows(1)
+    send_block(ROUND[1], 1)
+    send_block(ROUND[1], 0)
+    for i in range(2, 4):
         pack_rows(i)
-        send_block(ROUND[i], 1)
         send_block(ROUND[i], 0)
     got[view] = send[view]
 
@@ -276,7 +278,13 @@
             grid[0, 2 * j + i] = jnp.where(edge, jnp.where(high_half, high[i], low[i]), 0.0)
         return carry
 
+    def block_left(dx, dz):
+        v = at(dx, dz)
+        out_to(v, send.at[v], got.at[view], a_s, a_r).wait_send()
+
     lax.fori_loop(8, 16, est_pair, 0)
+    block_left(0, 1)
+    send_block(ROUND[2], 1)
     centre = grid[0, 16:32]
     grid[1, 16:32] = swap(centre)
     start_rims(volume_rim, 0, (0, 1))
@@ -308,6 +316,8 @@
         return carry
 
     lax.fori_loop(0, VIEWS, prepare, 0)
+    block_left(ROUND[1], 1)
+    send_block(ROUND[3], 1)
     for d in (0, 1):
         when(goes[d], lambda d=d: lit_copy(d).start())
 
@@ -357,9 +367,9 @@
     def blur_rims(v, carry):
         deep = dot3(depth_in[...], band_t[v])
         for s in range(2):
-            acc = blurred[v, :, 8 * s : 8 * s + 8] + deep[:, 8 * s : 8 * s + 8]
-            acc = tap_sum(acc, 0, 16, in_layout(v, 1, 15, s), -15, 1, v)
-            blurred[v, :, 8 * s : 8 * s + 8] = tap_sum(acc, 0, 16, in_layout(v, 32, 15, s), 16, 1, v)
+            acc = tap_sum(blurred[v, :, 8 * s : 8 * s + 8], 0, 16, in_layout(v, 1, 15, s), -15, 1, v)
+            acc = tap_sum(acc, 0, 16, in_layout(v, 32, 15, s), 16, 1, v)
+            blurred[v, :, 8 * s : 8 * s + 8] = acc + deep[:, 8 * s : 8 * s + 8]
         return carry
 
     lane3 = lane_of((16, 16, LANES))
@@ -373,7 +383,6 @@
         y = jnp.broadcast_to(flags_of[v, 1:2], (8, LANES))
         lit = jnp.broadcast_to(flags_of[v, 2:3], (8, LANES))
         deep = dot3(split3(ratio.reshape(256, LANES), (0, 0, 1)), band[v])
-        total[0, 16:32] += deep * lit[:1][None]
         for s in range(2):
             r = ratio[:, 8 * s : 8 * s + 8]
             for first, row in ((-HALF, 1), (16, 0)):
@@ -382,6 +391,7 @@
                 lit_x = jnp.broadcast_to(lit_got[row, pl.ds(v, 1)], (8, LANES))
                 total[1, cells, 8 * s : 8 * s + 8] += acc * (x * lit_x)[None]
                 total[0, cells, 8 * s : 8 * s + 8] += acc * (y * lit)[None]
+        total[0, 16:32] += deep * lit[:1][None]
 
     def spread_inside(v, carry):
         x = along_x(v)
@@ -435,7 +445,7 @@
     lax.fori_loop(1, VIEWS, spread_arrived, 0)
 
     def send_sums(phase):
-        start_rims(sum_rim, phase, range(4))
+        start_rims(sum_rim, phase, (2, 3, 0, 1))
         rim_send[phase] = pack_rim(total[0, 16:32].reshape(256, LANES), jnp.where(upper, 0, 16))
         start_rims(sum_rim, phase, (4,))
         lax.fori_loop(0, VIEWS, spread_inside, 0)
@@ -501,11 +511,7 @@
         for dx in (1, 3, 2):
             forward_copy(dx, i, mate).start()
 
-    def out_copy(i, rows):
-        cells = pl.ds(pl.multiple_of(rows * CHUNK, LANES), CHUNK)
-        return pltpu.make_async_copy(out.at[:, cells], out_hbm.at[:, cells], out_sem.at[i])
-
-    def unpack_out(i, rows):
+    def unpack_out(rows):
         for part in range(4):
             low = unpack([gathered[2 * rows + odd, 3 * part + j] for j in range(3)])
             high = unpack([gathered[2 * rows + 1 - odd, 3 * part + j] for j in range(3)])
@@ -513,22 +519,22 @@
             for p in range(2):
                 for j, t in enumerate(halves_pair(low[2 * p], high[2 * p], low[2 * p + 1], high[2 * p + 1])):
                     out[:, pl.ds(base + LANES * (3 * p + j), LANES)] = t
-        out_copy(i, rows).start()
-
-    unpack_out(0, cx)
-    for n, dx in enumerate((1, 3, 2)):
+
+    unpack_out(cx)
+    for dx in (1, 3, 2):
         source = at(XC - dx, 0)
         row_copy(dx, source).wait_recv()
         for i in range(PIECES):
             forward_copy(dx, i, at(XC - dx, 1)).wait_recv()
-        unpack_out(n + 1, source // 2)
+        unpack_out(source // 2)
 
     for d in (0, 1):
         when(goes[d], lambda d=d: lit_copy(d).wait_send())
     for dx, dz in others:
         v = at(dx, dz)
         out_to(v, tap_send.at[0], tap_got.at[view], t_s, t_r).wait_send()
-        out_to(v, send.at[v], got.at[view], a_s, a_r).wait_send()
+        if (dx, dz) not in ((0, 1), (ROUND[1], 1)):
+            block_left(dx, dz)
     sent_rims(volume_rim, 2, range(5))
     sent_rims(sum_rim, 3, range(5))
     for i in range(PIECES):
@@ -537,14 +543,12 @@
         row_copy(dx, view).wait_send()
         for i in range(PIECES):
             forward_copy(dx, i, mate).wait_send()
-    for i in range(4):
-        out_copy(i, cx).wait()
 
 
 def on_device(estimate, recorded, kernels, illuminated, detection):
     dma = pltpu.SemaphoreType.DMA
     vmem = lambda *shape: pltpu.VMEM(shape, F32)
-    any_space = pl.BlockSpec(memory_space=pl.ANY)
+    any_space = pl.BlockSpec(memory_space=pltpu.HBM)
     return pl.pallas_call(
         kernel,
         out_shape=jax.ShapeDtypeStruct((CX, YW * Z), F32),
@@ -555,11 +559,11 @@
             pl.BlockSpec(memory_space=pltpu.SMEM),
             pl.BlockSpec(memory_space=pltpu.SMEM),
         ],
-        out_specs=any_space,
+        out_specs=pl.BlockSpec(memory_space=pltpu.VMEM),
         scratch_shapes=[
             vmem(CX, YW * Z + 2 * CHUNK),
             vmem(CX, YW * Z),
-            vmem(TAPS, Z),
+            vmem(TAPS, 1, Z),
             vmem(VIEWS, PACKED, CX, LANES),
             vmem(VIEWS, PACKED, CX, LANES),
             vmem(2, 3, 8, LANES),
@@ -579,9 +583,7 @@
             vmem(4, 32, LANES),
             vmem(4, 32, LANES),
             vmem(VIEWS, PACKED, CX, LANES),
-            vmem(CX, YW * Z),
             dma((6,)),
-            dma((4,)),
             dma((VIEWS,)), dma((VIEWS,)),
             dma((VIEWS,)), dma((VIEWS,)),
             dma((2,)), dma((2,)),
@@ -593,7 +595,7 @@
         compiler_params=pltpu.CompilerParams(
             collective_id=0, has_side_effects=True, vmem_limit_bytes=VMEM_BYTES
         ),
-    )(estimate, recorded, kernels, illuminated, detection)
+    )(estimate, recorded, jnp.swapaxes(kernels, 0, 1), illuminated, detection)
 
 
 def solution(mesh):

time: 77.7 us -> 73.1 us (0.941)
  Pallas kernels: 72.7 us -> 70 us
  local copies, waits for them, and re-layouts: 3.44 us -> 1.63 us
    pallas_call x1, Pallas kernels: 72.7 us -> 70 us  [on_device(): pl.pallas_call(kernel, out_shape=jax.ShapeDtypeStruct((CX, YW * Z), F32),...]
    unnamed x2 -> x3, local copies, waits for them, and re-layouts: 3.44 us -> 1.63 us
where the time goes in v3:
time: 73.1 us; the launch traced here: 72.9 us
  Pallas kernels  70 us (96%)
  local copies, waits for them, and re-layouts  1.63 us (2%)
  between operations  1.31 us (2%)
    pallas_call x1, Pallas kernels, on_device(): pl.pallas_call(kernel, out_shape=jax.ShapeDtypeStruct((CX, YW * Z), F32),...  70 us
    unnamed x3, local copies, waits for them, and re-layouts  1.63 us

profile of v3, /device:TPU:32, one launch (start us, length us, event | category | flops | bytes accessed | tf_op | source)
XLA Modules:
  0.0 72.9 jit_solution(13592941562555403627)
XLA Ops:
  1.3 0.0 copy-start
  1.3 0.7 %copy-done = f32[1,31,192]{2,0,1:T(1,128)S(1)} copy-done((f32[1,31,192]{2,0,1:T(1,128)S(1)}, f32[1,31,192]{2,0,1:T(1,128)}, u32[]{:S(2)}) %copy-start) | copy-done | bytes 23832
  2.1 70.0 %shard_map.55 = f32[16,12288]{1,0:T(8,128)S(1)} custom-call(f32[16,12288]{1,0:T(8,128)} %est_hbm.1, f32[1,16,12288]{2,1,0:T(8,128)} %rec_hbm.1, f32[31,1,192]{2,1,0:T(1,128)S(1)} %bitcast.1, s32[1,1]{1,0:T(1,128)S(6)} %copy.7.lit_ref, s32[1]{0:T(128)S(6)} %copy.8.det_ref), custom_call_target="tpu_custom_call" | custom-call | tf_op jit(solution)/shard_map/pallas_call | solution.py:552
  72.0 0.9 %copy.9 = f32[16,12288]{1,0:T(8,128)} copy(f32[16,12288]{1,0:T(8,128)S(1)} %shard_map.55) | data formatting | bytes 1572864
Async XLA Ops:
  1.3 0.8 %copy-start = (f32[1,31,192]{2,0,1:T(1,128)S(1)}, f32[1,31,192]{2,0,1:T(1,128)}, u32[]{:S(2)}) copy-start(f32[1,31,192]{2,0,1:T(1,128)} %param.7) | copy-start | bytes 71428

commit v4 on v3

--- a/solution.py
+++ b/solution.py
@@ -87,16 +87,20 @@
     )
 
 
-def split3(a, order):
+def parts_of(a, order):
     high = a.astype(BF16)
     low = (a - high.astype(F32)).astype(BF16)
-    return jnp.concatenate([(high, low)[i] for i in order], axis=-1)
+    return [(high, low)[i] for i in order]
+
+
+def split3(a):
+    return jnp.concatenate(parts_of(a, (0, 0, 1)), axis=-1)
 
 
 def kernel(
     est_hbm, rec_hbm, ker_hbm, lit_ref, det_ref, out,
     est, rec, kpad, send, got, tap_send, tap_got, lit_send, lit_got, flags_of,
-    weight, band, band_t, grid, depth_in, rec_in, blurred, total, land, rim_send, rim_land, gathered,
+    weight, band, band_t, grid, depth_in, deep, ratios, rec_in, blurred, total, land, rim_send, rim_land, gathered,
     in_sem, a_s, a_r, t_s, t_r, l_s, l_r, h_s, h_r, g_s, g_r, z_s, z_r, f_s, f_r,
 ):
     view = lax.axis_index("view")
@@ -151,26 +155,31 @@
         rec_in_copy(i).start()
     est_copy.start()
 
-    def rim_copy(phase, d, src, dst):
+    def rim_copy(phase, d, src, dst, half=0):
         return pltpu.make_async_remote_copy(
-            src_ref=src, dst_ref=dst, send_sem=h_s.at[phase, d], recv_sem=h_r.at[phase, d],
+            src_ref=src, dst_ref=dst, send_sem=h_s.at[phase, d, half], recv_sem=h_r.at[phase, d, half],
             device_id=to_device[d], device_id_type=MESH,
         )
 
     def volume_rim(phase, d):
-        if d == 4:
-            return rim_copy(phase, d, rim_send.at[phase], rim_land.at[phase])
         layout = 1 if d < 2 else 0
         if d % 2 == 0:
             return rim_copy(phase, d, grid.at[layout, pl.ds(16, 15)], grid.at[layout, pl.ds(32, 15)])
         return rim_copy(phase, d, grid.at[layout, pl.ds(17, 15)], grid.at[layout, pl.ds(1, 15)])
 
-    def sum_rim(phase, d):
-        if d == 4:
-            return rim_copy(phase, d, rim_send.at[phase], rim_land.at[phase])
-        layout = 1 if d < 2 else 0
-        first = 1 if d % 2 == 0 else 32
-        return rim_copy(phase, d, total.at[layout, pl.ds(first, 15)], land.at[phase // 2, d])
+    def sum_rim(half):
+        def make(phase, d):
+            layout = 1 if d < 2 else 0
+            first = 1 if d % 2 == 0 else 32
+            part = pl.ds(8 * half, 8)
+            return rim_copy(
+                phase, d, total.at[layout, pl.ds(first, 15), part], land.at[phase // 2, d, :, part], half
+            )
+
+        return make
+
+    def depth_rim(phase, d):
+        return rim_copy(phase, d, rim_send.at[phase], rim_land.at[phase])
 
     def start_rims(make, phase, dirs):
         for d in dirs:
@@ -242,10 +251,7 @@
         v = at(dx, dz)
         out_to(v, tap_send.at[lax.rem(v + odd, 2)], tap_got.at[view], t_s, t_r).start()
     send_block(0, 1)
-    pack_rows(1)
-    send_block(ROUND[1], 1)
-    send_block(ROUND[1], 0)
-    for i in range(2, 4):
+    for i in range(1, 4):
         pack_rows(i)
         send_block(ROUND[i], 0)
     got[view] = send[view]
@@ -283,14 +289,15 @@
         out_to(v, send.at[v], got.at[view], a_s, a_r).wait_send()
 
     lax.fori_loop(8, 16, est_pair, 0)
-    block_left(0, 1)
-    send_block(ROUND[2], 1)
     centre = grid[0, 16:32]
     grid[1, 16:32] = swap(centre)
     start_rims(volume_rim, 0, (0, 1))
-    depth_in[...] = split3(centre.reshape(256, LANES), (0, 0, 1))
+    send_block(ROUND[1], 1)
+    depth_in[...] = split3(centre.reshape(256, LANES))
     lax.fori_loop(0, 8, est_pair, 0)
     lax.fori_loop(16, 24, est_pair, 0)
+    block_left(0, 1)
+    send_block(ROUND[2], 1)
 
     for dx, dz in others:
         v = at(dx, dz)
@@ -309,10 +316,13 @@
         flags_of[v] = jnp.concatenate([along[0], along[1], lit, jnp.zeros((5, LANES), F32)], axis=0)
         lit_send[pl.ds(v, 1)] = lit
         weight[v] = taps * (along[0] + along[1])
-        deep = jnp.concatenate([taps * along[2], jnp.zeros((LANES - 32, LANES), F32)], axis=0)
-        full = pltpu.roll(jnp.transpose(deep), LANES - HALF, 1, stride=1, stride_axis=0)
-        band[v] = split3(full, (0, 1, 0))
-        band_t[v] = split3(jnp.transpose(full), (0, 1, 0))
+        tall = jnp.concatenate([taps * along[2], jnp.zeros((LANES - 32, LANES), F32)], axis=0)
+        full = pltpu.roll(jnp.transpose(tall), LANES - HALF, 1, stride=1, stride_axis=0)
+        for i, part in enumerate(parts_of(full * lit, (0, 1, 0))):
+            band[pl.ds(pl.multiple_of(v * 3 * LANES + i * LANES, LANES), LANES)] = part
+        here = pl.ds(pl.multiple_of(v * LANES, LANES), LANES)
+        for i, part in enumerate(parts_of(jnp.transpose(full), (0, 1, 0))):
+            band_t[LANES * i : LANES * (i + 1), here] = part
         return carry
 
     lax.fori_loop(0, VIEWS, prepare, 0)
@@ -321,13 +331,14 @@
     for d in (0, 1):
         when(goes[d], lambda d=d: lit_copy(d).start())
 
-    def dot3(a, parts):
-        out = jnp.zeros((256, LANES), F32)
-        for i in range(3):
-            out += jnp.dot(
-                a[:, LANES * i : LANES * (i + 1)], parts[:, LANES * i : LANES * (i + 1)], preferred_element_type=F32
-            )
-        return out.reshape(16, 16, LANES)
+    def depth_products():
+        product = jnp.dot(depth_in[...], band_t[...], preferred_element_type=F32)
+        for v in range(VIEWS):
+            deep[v] = product[:, LANES * v : LANES * (v + 1)].reshape(16, 16, LANES)
+
+    def depth_sums():
+        product = jnp.dot(ratios[...], band[...], preferred_element_type=F32)
+        total[0, 16:32] += product.reshape(16, 16, LANES)
 
     def tap_sum(out, first, count, source, origin, sign, v):
         length = source.shape[0]
@@ -365,33 +376,32 @@
         return carry
 
     def blur_rims(v, carry):
-        deep = dot3(depth_in[...], band_t[v])
         for s in range(2):
             acc = tap_sum(blurred[v, :, 8 * s : 8 * s + 8], 0, 16, in_layout(v, 1, 15, s), -15, 1, v)
             acc = tap_sum(acc, 0, 16, in_layout(v, 32, 15, s), 16, 1, v)
-            blurred[v, :, 8 * s : 8 * s + 8] = acc + deep[:, 8 * s : 8 * s + 8]
+            blurred[v, :, 8 * s : 8 * s + 8] = acc + deep[v, :, 8 * s : 8 * s + 8]
         return carry
 
     lane3 = lane_of((16, 16, LANES))
     inner3 = (lane3 >= RIM) & (lane3 < RIM + DEPTH)
 
-    def spread_rims(v):
+    def take_ratio(v):
         first_dim = jnp.broadcast_to((along_x(v) > 0.5)[None, :1], (16, 16, LANES))
         ratio = jnp.where(inner3, jnp.where(first_dim, rec_in[1, v], rec_in[0, v]) / blurred[v], 0.0)
         blurred[v] = ratio
+        ratios[:, pl.ds(pl.multiple_of(v * 3 * LANES, LANES), 3 * LANES)] = split3(ratio.reshape(256, LANES))
+
+    def spread_rims(v, s):
         x = along_x(v)
         y = jnp.broadcast_to(flags_of[v, 1:2], (8, LANES))
         lit = jnp.broadcast_to(flags_of[v, 2:3], (8, LANES))
-        deep = dot3(split3(ratio.reshape(256, LANES), (0, 0, 1)), band[v])
-        for s in range(2):
-            r = ratio[:, 8 * s : 8 * s + 8]
-            for first, row in ((-HALF, 1), (16, 0)):
-                acc = tap_sum(jnp.zeros((HALF, 8, LANES), F32), first, HALF, r, 0, -1, v)
-                cells = slice(first + 16, first + 16 + HALF)
-                lit_x = jnp.broadcast_to(lit_got[row, pl.ds(v, 1)], (8, LANES))
-                total[1, cells, 8 * s : 8 * s + 8] += acc * (x * lit_x)[None]
-                total[0, cells, 8 * s : 8 * s + 8] += acc * (y * lit)[None]
-        total[0, 16:32] += deep * lit[:1][None]
+        r = blurred[v, :, 8 * s : 8 * s + 8]
+        for first, row in ((-HALF, 1), (16, 0)):
+            acc = tap_sum(jnp.zeros((HALF, 8, LANES), F32), first, HALF, r, 0, -1, v)
+            cells = slice(first + 16, first + 16 + HALF)
+            lit_x = jnp.broadcast_to(lit_got[row, pl.ds(v, 1)], (8, LANES))
+            total[1, cells, 8 * s : 8 * s + 8] += acc * (x * lit_x)[None]
+            total[0, cells, 8 * s : 8 * s + 8] += acc * (y * lit)[None]
 
     def spread_inside(v, carry):
         x = along_x(v)
@@ -418,6 +428,7 @@
         return jnp.where(inner3, grid[0, 16:32] * summed * (1.0 / VIEWS), 0.0)
 
     lax.fori_loop(0, VIEWS, blur_inside, 0)
+    depth_products()
     recv_rims(volume_rim, 0, (0, 1))
     lax.fori_loop(0, VIEWS, blur_rims, 0)
     for d in (0, 1):
@@ -432,48 +443,77 @@
 
     total[...] = jnp.zeros((2, 48, 16, LANES), F32)
     arrive(view)
-    spread_rims(view)
+    take_ratio(view)
+    for s in range(2):
+        spread_rims(view, s)
 
     def spread_arrived(step, carry):
-        order = lax.rem(step, 4)
+        i = lax.rem(step, 4)
+        order = jnp.where(i == 0, 0, lax.rem(i + 1, 3) + 1)
         v = lax.rem(cx + order, XC) * 2 + lax.rem(zh + step // 4, 2)
         from_view(v, got.at[v], a_r).wait_recv()
         arrive(v)
-        spread_rims(v)
+        take_ratio(v)
+        for s in range(2):
+            spread_rims(v, s)
         return carry
 
     lax.fori_loop(1, VIEWS, spread_arrived, 0)
 
-    def send_sums(phase):
-        start_rims(sum_rim, phase, (2, 3, 0, 1))
+    SIDES = (2, 3, 0, 1)
+
+    def send_depth_sums(phase):
+        depth_sums()
         rim_send[phase] = pack_rim(total[0, 16:32].reshape(256, LANES), jnp.where(upper, 0, 16))
-        start_rims(sum_rim, phase, (4,))
+        start_rims(depth_rim, phase, (4,))
+
+    def finish_sums(phase):
         lax.fori_loop(0, VIEWS, spread_inside, 0)
-        recv_rims(sum_rim, phase, range(5))
+        for half in range(2):
+            recv_rims(sum_rim(half), phase, SIDES)
+        recv_rims(depth_rim, phase, (4,))
+
+    def sums_left(phase):
+        for half in range(2):
+            sent_rims(sum_rim(half), phase, SIDES)
+        sent_rims(depth_rim, phase, (4,))
 
     sent_rims(volume_rim, 0, (0, 1))
-    send_sums(1)
+    for half in range(2):
+        start_rims(sum_rim(half), 1, SIDES)
+    send_depth_sums(1)
+    finish_sums(1)
     fresh = update(1)
     grid[0, 16:32] = fresh
     start_rims(volume_rim, 2, (2, 3))
     grid[1, 16:32] = swap(fresh)
     start_rims(volume_rim, 2, (0, 1))
     rim_send[2] = pack_rim(fresh.reshape(256, LANES), jnp.where(upper, 112, 32))
-    start_rims(volume_rim, 2, (4,))
-    sent_rims(sum_rim, 1, range(5))
+    start_rims(depth_rim, 2, (4,))
+    sums_left(1)
     total[...] = jnp.zeros((2, 48, 16, LANES), F32)
     lax.fori_loop(0, VIEWS, blur_inside, 0)
-    recv_rims(volume_rim, 2, range(5))
+    recv_rims(depth_rim, 2, (4,))
     deep_rim = unpack_rim(rim_land[2], jnp.where(upper, 0, 112))
-    depth_in[...] = split3(grid[0, 16:32].reshape(256, LANES) + deep_rim, (0, 0, 1))
+    depth_in[...] = split3(grid[0, 16:32].reshape(256, LANES) + deep_rim)
+    depth_products()
+    recv_rims(volume_rim, 2, SIDES)
 
     def second(v, carry):
         blur_rims(v, 0)
-        spread_rims(v)
+        take_ratio(v)
         return carry
 
     lax.fori_loop(0, VIEWS, second, 0)
-    send_sums(3)
+    send_depth_sums(3)
+    for half in range(2):
+        def beyond(v, carry, half=half):
+            spread_rims(v, half)
+            return carry
+
+        lax.fori_loop(0, VIEWS, beyond, 0)
+        start_rims(sum_rim(half), 3, SIDES)
+    finish_sums(3)
     fresh = update(3)
 
     for part in range(4):
@@ -535,8 +575,9 @@
         out_to(v, tap_send.at[0], tap_got.at[view], t_s, t_r).wait_send()
         if (dx, dz) not in ((0, 1), (ROUND[1], 1)):
             block_left(dx, dz)
-    sent_rims(volume_rim, 2, range(5))
-    sent_rims(sum_rim, 3, range(5))
+    sent_rims(volume_rim, 2, SIDES)
+    sent_rims(depth_rim, 2, (4,))
+    sums_left(3)
     for i in range(PIECES):
         half_copy(i, view).wait_send()
     for dx in (1, 3, 2):
@@ -572,10 +613,12 @@
             vmem(2, 8, LANES),
             vmem(VIEWS, 8, LANES),
             vmem(VIEWS, 32, LANES),
-            pltpu.VMEM((VIEWS, LANES, 3 * LANES), BF16),
-            pltpu.VMEM((VIEWS, LANES, 3 * LANES), BF16),
+            pltpu.VMEM((VIEWS * 3 * LANES, LANES), BF16),
+            pltpu.VMEM((3 * LANES, VIEWS * LANES), BF16),
             vmem(2, 48, 16, LANES),
             pltpu.VMEM((256, 3 * LANES), BF16),
+            vmem(VIEWS, 16, 16, LANES),
+            pltpu.VMEM((256, VIEWS * 3 * LANES), BF16),
             vmem(2, VIEWS, 16, 16, LANES),
             vmem(VIEWS, 16, 16, LANES),
             vmem(2, 48, 16, LANES),
@@ -587,7 +630,7 @@
             dma((VIEWS,)), dma((VIEWS,)),
             dma((VIEWS,)), dma((VIEWS,)),
             dma((2,)), dma((2,)),
-            dma((4, 5)), dma((4, 5)),
+            dma((4, 5, 2)), dma((4, 5, 2)),
             dma((3,)), dma((3,)),
             dma((PIECES,)), dma((PIECES,)),
             dma((3, PIECES)), dma((3, PIECES)),

time: 73.1 us -> 70.8 us (0.969)
  Pallas kernels: 70 us -> 66.9 us
    pallas_call x1, Pallas kernels: 70 us -> 66.9 us  [on_device(): pl.pallas_call(kernel, out_shape=jax.ShapeDtypeStruct((CX, YW * Z), F32),...]
where the time goes in v4:
time: 70.8 us; the launch traced here: 69.9 us
  Pallas kernels  66.9 us (94%)
  local copies, waits for them, and re-layouts  1.63 us (2%)
  between operations  1.31 us (2%)
    pallas_call x1, Pallas kernels, on_device(): pl.pallas_call(kernel, out_shape=jax.ShapeDtypeStruct((CX, YW * Z), F32),...  66.9 us
    unnamed x3, local copies, waits for them, and re-layouts  1.63 us

profile of v4, /device:TPU:32, one launch (start us, length us, event | category | flops | bytes accessed | tf_op | source)
XLA Modules:
  0.0 69.9 jit_solution(1437552896345386636)
XLA Ops:
  1.3 0.0 copy-start
  1.3 0.7 %copy-done = f32[1,31,192]{2,0,1:T(1,128)S(1)} copy-done((f32[1,31,192]{2,0,1:T(1,128)S(1)}, f32[1,31,192]{2,0,1:T(1,128)}, u32[]{:S(2)}) %copy-start) | copy-done | bytes 23832
  2.1 66.9 %shard_map.55 = f32[16,12288]{1,0:T(8,128)S(1)} custom-call(f32[16,12288]{1,0:T(8,128)} %est_hbm.1, f32[1,16,12288]{2,1,0:T(8,128)} %rec_hbm.1, f32[31,1,192]{2,1,0:T(1,128)S(1)} %bitcast.1, s32[1,1]{1,0:T(1,128)S(6)} %copy.7.lit_ref, s32[1]{0:T(128)S(6)} %copy.8.det_ref), custom_call_target="tpu_custom_call" | custom-call | tf_op jit(solution)/shard_map/pallas_call | solution.py:593
  69.0 0.9 %copy.9 = f32[16,12288]{1,0:T(8,128)} copy(f32[16,12288]{1,0:T(8,128)S(1)} %shard_map.55) | data formatting | bytes 1572864
Async XLA Ops:
  1.3 0.8 %copy-start = (f32[1,31,192]{2,0,1:T(1,128)S(1)}, f32[1,31,192]{2,0,1:T(1,128)}, u32[]{:S(2)}) copy-start(f32[1,31,192]{2,0,1:T(1,128)} %param.7) | copy-start | bytes 71428

commit v5 on v4

--- a/solution.py
+++ b/solution.py
@@ -99,14 +99,16 @@
 
 def kernel(
     est_hbm, rec_hbm, ker_hbm, lit_ref, det_ref, out,
-    est, rec, kpad, send, got, tap_send, tap_got, lit_send, lit_got, flags_of,
+    est, rec, kpad, send, got, tap_send, tap_got, lit_of, lit_got, flags_of,
     weight, band, band_t, grid, depth_in, deep, ratios, rec_in, blurred, total, land, rim_send, rim_land, gathered,
-    in_sem, a_s, a_r, t_s, t_r, l_s, l_r, h_s, h_r, g_s, g_r, z_s, z_r, f_s, f_r,
+    in_sem, a_s, a_r, t_s, t_r, m_s, m_r, e_s, e_r, l_s, l_r, h_s, h_r, g_s, g_r, z_s, z_r, f_s, f_r,
 ):
     view = lax.axis_index("view")
     tile = lax.axis_index("tile")
     cx, zh = view // 2, lax.rem(view, 2)
     odd = lax.rem(tile // 8, 2)
+    core = lax.rem(tile, 2)
+    chip_mate = (view, tile + 1 - 2 * core)
     deep_half = lax.rem(zh + odd, 2)
     upper = deep_half == 1
 
@@ -205,7 +207,7 @@
 
     def lit_copy(d):
         return pltpu.make_async_remote_copy(
-            src_ref=lit_send, dst_ref=lit_got.at[d], send_sem=l_s.at[d], recv_sem=l_r.at[d],
+            src_ref=lit_of, dst_ref=lit_got.at[d], send_sem=l_s.at[d], recv_sem=l_r.at[d],
             device_id=to_device[d], device_id_type=MESH,
         )
 
@@ -214,16 +216,16 @@
     row32 = lax.broadcasted_iota(jnp.int32, (32, LANES), 0)
     axis_now = det_ref[0].astype(F32)
     lit_now = (lit_ref[0, 0] > 0).astype(F32)
-    flags = jnp.where(lane32 < 48, axis_now, lit_now)
     k0 = jnp.concatenate([kpad[:, 0, 0:LANES], jnp.zeros((1, LANES), F32)], axis=0)
     k1 = jnp.concatenate([kpad[:, 0, LANES:Z], jnp.zeros((TAPS, 2 * LANES - Z), F32)], axis=1)
     k1 = jnp.concatenate([k1, jnp.zeros((1, LANES), F32)], axis=0)
     for half in range(2):
         taps = roll(k0, 16) if half == 0 else jnp.where(lane32 < 48, roll(k0, 48), roll(k1, 48))
-        taps = jnp.where(row32 == TAPS, flags, taps)
+        taps = jnp.where(row32 == TAPS, axis_now, taps)
         for i, t in enumerate(pack([taps[8 * j : 8 * j + 8] for j in range(4)])):
             tap_send[half, i] = t
     tap_got[view] = tap_send[deep_half]
+    lit_of[view] = jnp.full((1, LANES), lit_now, F32)
 
     def pack_rows(i):
         rec_in_copy(i).wait()
@@ -247,10 +249,25 @@
 
     pack_rows(0)
     pl.semaphore_wait(barrier, 7 + (tile > 0).astype(jnp.int32) + (tile < TILES - 1).astype(jnp.int32))
+
+    FAR = ((0, 0), (1, 1), (3, 0), (2, 1))
+
+    def tap_copy(v):
+        return out_to(v, tap_send.at[lax.rem(v + odd, 2)], tap_got.at[view], t_s, t_r)
+
+    def tap_pass(v):
+        return pltpu.make_async_remote_copy(
+            src_ref=tap_got.at[v], dst_ref=tap_got.at[v], send_sem=m_s.at[v], recv_sem=m_r.at[v],
+            device_id=chip_mate, device_id_type=MESH,
+        )
+
+    for dx, c in FAR:
+        pl.when(core == c)(lambda dx=dx: tap_copy(at(dx, 1)).start())
+    send_block(0, 1)
+    for dx in (1, 3, 2):
+        tap_copy(at(dx, 0)).start()
     for dx, dz in others:
-        v = at(dx, dz)
-        out_to(v, tap_send.at[lax.rem(v + odd, 2)], tap_got.at[view], t_s, t_r).start()
-    send_block(0, 1)
+        out_to(at(dx, dz), lit_of.at[view], lit_of.at[view], e_s, e_r).start()
     for i in range(1, 4):
         pack_rows(i)
         send_block(ROUND[i], 0)
@@ -261,7 +278,7 @@
         @pl.when(jnp.logical_not(comes[d]))
         def _(d=d, into=into):
             grid[1, into : into + 16] = zero_rim
-            lit_got[d] = jnp.zeros((8, LANES), F32)
+            lit_got[d] = jnp.zeros((VIEWS, 1, LANES), F32)
 
     for d in range(4):
         @pl.when(jnp.logical_not(comes[d]))
@@ -291,43 +308,54 @@
     lax.fori_loop(8, 16, est_pair, 0)
     centre = grid[0, 16:32]
     grid[1, 16:32] = swap(centre)
+    send_block(ROUND[1], 1)
     start_rims(volume_rim, 0, (0, 1))
-    send_block(ROUND[1], 1)
+    send_block(ROUND[2], 1)
+    send_block(ROUND[3], 1)
     depth_in[...] = split3(centre.reshape(256, LANES))
     lax.fori_loop(0, 8, est_pair, 0)
     lax.fori_loop(16, 24, est_pair, 0)
-    block_left(0, 1)
-    send_block(ROUND[2], 1)
-
+
+    for dx, c in FAR:
+        def take_far(dx=dx):
+            v = at(XC - dx, 1)
+            from_view(v, tap_got.at[v], t_r).wait_recv()
+            tap_pass(v).start()
+
+        pl.when(core == c)(take_far)
+    for dx in (1, 3, 2):
+        v = at(dx, 0)
+        from_view(v, tap_got.at[v], t_r).wait_recv()
     for dx, dz in others:
         v = at(dx, dz)
-        from_view(v, tap_got.at[v], t_r).wait_recv()
+        from_view(v, lit_of.at[v], e_r).wait_recv()
+    for dx, c in FAR:
+        pl.when(core != c)(lambda dx=dx: tap_pass(at(XC - dx, 1)).wait_recv())
+
+    def slot(v):
+        return lax.rem(v + zh, 2) * XC + v // 2
 
     def prepare(v, carry):
         taps = jnp.concatenate(unpack([tap_got[v, i] for i in range(3)]), axis=0)
         marks = taps[31:32]
         lane = lane_of((1, LANES))
         axis = jnp.sum(jnp.where(lane == 32, marks, 0.0), axis=1, keepdims=True)
-        lit = jnp.sum(jnp.where(lane == 64, marks, 0.0), axis=1, keepdims=True)
+        lit = lit_of[v]
         inner = (lane32 >= RIM) & (lane32 < RIM + DEPTH) & (row32 < TAPS)
         taps = jnp.where(inner, taps, 0.0)
         along = [jnp.broadcast_to(jnp.where(axis == float(d), 1.0, 0.0), (1, LANES)) for d in range(3)]
-        lit = jnp.broadcast_to(lit, (1, LANES))
         flags_of[v] = jnp.concatenate([along[0], along[1], lit, jnp.zeros((5, LANES), F32)], axis=0)
-        lit_send[pl.ds(v, 1)] = lit
         weight[v] = taps * (along[0] + along[1])
         tall = jnp.concatenate([taps * along[2], jnp.zeros((LANES - 32, LANES), F32)], axis=0)
         full = pltpu.roll(jnp.transpose(tall), LANES - HALF, 1, stride=1, stride_axis=0)
         for i, part in enumerate(parts_of(full * lit, (0, 1, 0))):
-            band[pl.ds(pl.multiple_of(v * 3 * LANES + i * LANES, LANES), LANES)] = part
+            band[pl.ds(pl.multiple_of(slot(v) * 3 * LANES + i * LANES, LANES), LANES)] = part
         here = pl.ds(pl.multiple_of(v * LANES, LANES), LANES)
         for i, part in enumerate(parts_of(jnp.transpose(full), (0, 1, 0))):
             band_t[LANES * i : LANES * (i + 1), here] = part
         return carry
 
     lax.fori_loop(0, VIEWS, prepare, 0)
-    block_left(ROUND[1], 1)
-    send_block(ROUND[3], 1)
     for d in (0, 1):
         when(goes[d], lambda d=d: lit_copy(d).start())
 
@@ -336,8 +364,9 @@
         for v in range(VIEWS):
             deep[v] = product[:, LANES * v : LANES * (v + 1)].reshape(16, 16, LANES)
 
-    def depth_sums():
-        product = jnp.dot(ratios[...], band[...], preferred_element_type=F32)
+    def depth_sums(part):
+        span = slice(part * XC * 3 * LANES, (part + 1) * XC * 3 * LANES)
+        product = jnp.dot(ratios[:, span], band[span], preferred_element_type=F32)
         total[0, 16:32] += product.reshape(16, 16, LANES)
 
     def tap_sum(out, first, count, source, origin, sign, v):
@@ -389,7 +418,7 @@
         first_dim = jnp.broadcast_to((along_x(v) > 0.5)[None, :1], (16, 16, LANES))
         ratio = jnp.where(inner3, jnp.where(first_dim, rec_in[1, v], rec_in[0, v]) / blurred[v], 0.0)
         blurred[v] = ratio
-        ratios[:, pl.ds(pl.multiple_of(v * 3 * LANES, LANES), 3 * LANES)] = split3(ratio.reshape(256, LANES))
+        ratios[:, pl.ds(pl.multiple_of(slot(v) * 3 * LANES, LANES), 3 * LANES)] = split3(ratio.reshape(256, LANES))
 
     def spread_rims(v, s):
         x = along_x(v)
@@ -399,7 +428,7 @@
         for first, row in ((-HALF, 1), (16, 0)):
             acc = tap_sum(jnp.zeros((HALF, 8, LANES), F32), first, HALF, r, 0, -1, v)
             cells = slice(first + 16, first + 16 + HALF)
-            lit_x = jnp.broadcast_to(lit_got[row, pl.ds(v, 1)], (8, LANES))
+            lit_x = jnp.broadcast_to(lit_got[row, v], (8, LANES))
             total[1, cells, 8 * s : 8 * s + 8] += acc * (x * lit_x)[None]
             total[0, cells, 8 * s : 8 * s + 8] += acc * (y * lit)[None]
 
@@ -447,23 +476,31 @@
     for s in range(2):
         spread_rims(view, s)
 
-    def spread_arrived(step, carry):
+    def view_of(step):
         i = lax.rem(step, 4)
         order = jnp.where(i == 0, 0, lax.rem(i + 1, 3) + 1)
-        v = lax.rem(cx + order, XC) * 2 + lax.rem(zh + step // 4, 2)
+        return lax.rem(cx + order, XC) * 2 + lax.rem(zh + step // 4, 2)
+
+    def take_arrived(step, carry):
+        v = view_of(step)
         from_view(v, got.at[v], a_r).wait_recv()
         arrive(v)
         take_ratio(v)
+        return carry
+
+    def spread_arrived(step, carry):
+        take_arrived(step, carry)
         for s in range(2):
-            spread_rims(v, s)
+            spread_rims(view_of(step), s)
         return carry
 
-    lax.fori_loop(1, VIEWS, spread_arrived, 0)
+    lax.fori_loop(1, XC, spread_arrived, 0)
+    depth_sums(0)
+    lax.fori_loop(XC, VIEWS, take_arrived, 0)
 
     SIDES = (2, 3, 0, 1)
 
     def send_depth_sums(phase):
-        depth_sums()
         rim_send[phase] = pack_rim(total[0, 16:32].reshape(256, LANES), jnp.where(upper, 0, 16))
         start_rims(depth_rim, phase, (4,))
 
@@ -478,10 +515,19 @@
             sent_rims(sum_rim(half), phase, SIDES)
         sent_rims(depth_rim, phase, (4,))
 
+    def spread_halves(phase, first):
+        for half in range(2):
+            def beyond(step, carry, half=half):
+                spread_rims(view_of(step), half)
+                return carry
+
+            lax.fori_loop(first, VIEWS, beyond, 0)
+            start_rims(sum_rim(half), phase, SIDES)
+
     sent_rims(volume_rim, 0, (0, 1))
-    for half in range(2):
-        start_rims(sum_rim(half), 1, SIDES)
+    depth_sums(1)
     send_depth_sums(1)
+    spread_halves(1, XC)
     finish_sums(1)
     fresh = update(1)
     grid[0, 16:32] = fresh
@@ -505,14 +551,10 @@
         return carry
 
     lax.fori_loop(0, VIEWS, second, 0)
+    depth_sums(0)
+    depth_sums(1)
     send_depth_sums(3)
-    for half in range(2):
-        def beyond(v, carry, half=half):
-            spread_rims(v, half)
-            return carry
-
-        lax.fori_loop(0, VIEWS, beyond, 0)
-        start_rims(sum_rim(half), 3, SIDES)
+    spread_halves(3, 0)
     finish_sums(3)
     fresh = update(3)
 
@@ -572,9 +614,13 @@
         when(goes[d], lambda d=d: lit_copy(d).wait_send())
     for dx, dz in others:
         v = at(dx, dz)
-        out_to(v, tap_send.at[0], tap_got.at[view], t_s, t_r).wait_send()
-        if (dx, dz) not in ((0, 1), (ROUND[1], 1)):
-            block_left(dx, dz)
+        out_to(v, lit_of.at[view], lit_of.at[view], e_s, e_r).wait_send()
+        block_left(dx, dz)
+    for dx, c in FAR:
+        pl.when(core == c)(lambda dx=dx: tap_copy(at(dx, 1)).wait_send())
+        pl.when(core == c)(lambda dx=dx: tap_pass(at(XC - dx, 1)).wait_send())
+    for dx in (1, 3, 2):
+        tap_copy(at(dx, 0)).wait_send()
     sent_rims(volume_rim, 2, SIDES)
     sent_rims(depth_rim, 2, (4,))
     sums_left(3)
@@ -609,8 +655,8 @@
             vmem(VIEWS, PACKED, CX, LANES),
             vmem(2, 3, 8, LANES),
             vmem(VIEWS, 3, 8, LANES),
-            vmem(8, LANES),
-            vmem(2, 8, LANES),
+            vmem(VIEWS, 1, LANES),
+            vmem(2, VIEWS, 1, LANES),
             vmem(VIEWS, 8, LANES),
             vmem(VIEWS, 32, LANES),
             pltpu.VMEM((VIEWS * 3 * LANES, LANES), BF16),
@@ -629,6 +675,8 @@
             dma((6,)),
             dma((VIEWS,)), dma((VIEWS,)),
             dma((VIEWS,)), dma((VIEWS,)),
+            dma((VIEWS,)), dma((VIEWS,)),
+            dma((VIEWS,)), dma((VIEWS,)),
             dma((2,)), dma((2,)),
             dma((4, 5, 2)), dma((4, 5, 2)),
             dma((3,)), dma((3,)),

time: 70.8 us -> 68.2 us (0.963)
  Pallas kernels: 66.9 us -> 64.5 us
    pallas_call x1, Pallas kernels: 66.9 us -> 64.5 us  [on_device(): pl.pallas_call(kernel, out_shape=jax.ShapeDtypeStruct((CX, YW * Z), F32),...]
where the time goes in v5:
time: 68.2 us; the launch traced here: 67.4 us
  Pallas kernels  64.5 us (95%)
  local copies, waits for them, and re-layouts  1.63 us (2%)
  between operations  1.31 us (2%)
    pallas_call x1, Pallas kernels, on_device(): pl.pallas_call(kernel, out_shape=jax.ShapeDtypeStruct((CX, YW * Z), F32),...  64.5 us
    unnamed x3, local copies, waits for them, and re-layouts  1.63 us

profile of v5, /device:TPU:32, one launch (start us, length us, event | category | flops | bytes accessed | tf_op | source)
XLA Modules:
  0.0 67.4 jit_solution(11937767420989601747)
XLA Ops:
  1.3 0.0 copy-start
  1.3 0.7 %copy-done = f32[1,31,192]{2,0,1:T(1,128)S(1)} copy-done((f32[1,31,192]{2,0,1:T(1,128)S(1)}, f32[1,31,192]{2,0,1:T(1,128)}, u32[]{:S(2)}) %copy-start) | copy-done | bytes 23832
  2.1 64.5 %shard_map.55 = f32[16,12288]{1,0:T(8,128)S(1)} custom-call(f32[16,12288]{1,0:T(8,128)} %est_hbm.1, f32[1,16,12288]{2,1,0:T(8,128)} %rec_hbm.1, f32[31,1,192]{2,1,0:T(1,128)S(1)} %bitcast.1, s32[1,1]{1,0:T(1,128)S(6)} %copy.7.lit_ref, s32[1]{0:T(128)S(6)} %copy.8.det_ref), custom_call_target="tpu_custom_call" | custom-call | tf_op jit(solution)/shard_map/pallas_call | solution.py:639
  66.5 0.9 %copy.9 = f32[16,12288]{1,0:T(8,128)} copy(f32[16,12288]{1,0:T(8,128)S(1)} %shard_map.55) | data formatting | bytes 1572864
Async XLA Ops:
  1.3 0.8 %copy-start = (f32[1,31,192]{2,0,1:T(1,128)S(1)}, f32[1,31,192]{2,0,1:T(1,128)}, u32[]{:S(2)}) copy-start(f32[1,31,192]{2,0,1:T(1,128)} %param.7) | copy-start | bytes 71428

commit v6 on v5

--- a/solution.py
+++ b/solution.py
@@ -1,3 +1,5 @@
+import functools
+
 import jax
 import jax.numpy as jnp
 from jax import lax
@@ -163,11 +165,16 @@
             device_id=to_device[d], device_id_type=MESH,
         )
 
-    def volume_rim(phase, d):
-        layout = 1 if d < 2 else 0
-        if d % 2 == 0:
-            return rim_copy(phase, d, grid.at[layout, pl.ds(16, 15)], grid.at[layout, pl.ds(32, 15)])
-        return rim_copy(phase, d, grid.at[layout, pl.ds(17, 15)], grid.at[layout, pl.ds(1, 15)])
+    def volume_rim(half):
+        def make(phase, d):
+            layout = 1 if d < 2 else 0
+            source, target = (16, 32) if d % 2 == 0 else (17, 1)
+            part = pl.ds(8 * half, 8)
+            return rim_copy(
+                phase, d, grid.at[layout, pl.ds(source, 15), part], grid.at[layout, pl.ds(target, 15), part], half
+            )
+
+        return make
 
     def sum_rim(half):
         def make(phase, d):
@@ -268,7 +275,10 @@
         tap_copy(at(dx, 0)).start()
     for dx, dz in others:
         out_to(at(dx, dz), lit_of.at[view], lit_of.at[view], e_s, e_r).start()
-    for i in range(1, 4):
+    pack_rows(1)
+    send_block(ROUND[1], 1)
+    send_block(ROUND[1], 0)
+    for i in range(2, 4):
         pack_rows(i)
         send_block(ROUND[i], 0)
     got[view] = send[view]
@@ -308,8 +318,8 @@
     lax.fori_loop(8, 16, est_pair, 0)
     centre = grid[0, 16:32]
     grid[1, 16:32] = swap(centre)
-    send_block(ROUND[1], 1)
-    start_rims(volume_rim, 0, (0, 1))
+    for half in range(2):
+        start_rims(volume_rim(half), 0, (0, 1))
     send_block(ROUND[2], 1)
     send_block(ROUND[3], 1)
     depth_in[...] = split3(centre.reshape(256, LANES))
@@ -404,19 +414,17 @@
             )
         return carry
 
-    def blur_rims(v, carry):
-        for s in range(2):
-            acc = tap_sum(blurred[v, :, 8 * s : 8 * s + 8], 0, 16, in_layout(v, 1, 15, s), -15, 1, v)
-            acc = tap_sum(acc, 0, 16, in_layout(v, 32, 15, s), 16, 1, v)
-            blurred[v, :, 8 * s : 8 * s + 8] = acc + deep[v, :, 8 * s : 8 * s + 8]
+    def blur_rims(s, v, carry):
+        acc = tap_sum(blurred[v, :, 8 * s : 8 * s + 8], 0, 16, in_layout(v, 1, 15, s), -15, 1, v)
+        acc = tap_sum(acc, 0, 16, in_layout(v, 32, 15, s), 16, 1, v)
+        blurred[v, :, 8 * s : 8 * s + 8] = acc + deep[v, :, 8 * s : 8 * s + 8]
         return carry
 
     lane3 = lane_of((16, 16, LANES))
     inner3 = (lane3 >= RIM) & (lane3 < RIM + DEPTH)
 
     def take_ratio(v):
-        first_dim = jnp.broadcast_to((along_x(v) > 0.5)[None, :1], (16, 16, LANES))
-        ratio = jnp.where(inner3, jnp.where(first_dim, rec_in[1, v], rec_in[0, v]) / blurred[v], 0.0)
+        ratio = jnp.where(inner3, rec_in[v] / blurred[v], 0.0)
         blurred[v] = ratio
         ratios[:, pl.ds(pl.multiple_of(slot(v) * 3 * LANES, LANES), 3 * LANES)] = split3(ratio.reshape(256, LANES))
 
@@ -458,17 +466,19 @@
 
     lax.fori_loop(0, VIEWS, blur_inside, 0)
     depth_products()
-    recv_rims(volume_rim, 0, (0, 1))
-    lax.fori_loop(0, VIEWS, blur_rims, 0)
+    for half in range(2):
+        recv_rims(volume_rim(half), 0, (0, 1))
+        lax.fori_loop(0, VIEWS, functools.partial(blur_rims, half), 0)
     for d in (0, 1):
         when(comes[d], lambda d=d: lit_copy(d).wait_recv())
 
     def arrive(v):
+        rows = []
         for part in range(4):
-            rows = unpack([got[v, 3 * part + i] for i in range(3)])
-            for i in range(4):
-                rec_in[0, v, 4 * part + i] = rows[i]
-        rec_in[1, v] = swap(rec_in[0, v])
+            rows += unpack([got[v, 3 * part + i] for i in range(3)])
+        cells = jnp.stack(rows)
+        first_dim = jnp.broadcast_to((along_x(v) > 0.5)[None, :1], (16, 16, LANES))
+        rec_in[v] = jnp.where(first_dim, swap(cells), cells)
 
     total[...] = jnp.zeros((2, 48, 16, LANES), F32)
     arrive(view)
@@ -524,18 +534,20 @@
             lax.fori_loop(first, VIEWS, beyond, 0)
             start_rims(sum_rim(half), phase, SIDES)
 
-    sent_rims(volume_rim, 0, (0, 1))
+    for half in range(2):
+        sent_rims(volume_rim(half), 0, (0, 1))
     depth_sums(1)
     send_depth_sums(1)
     spread_halves(1, XC)
     finish_sums(1)
     fresh = update(1)
     grid[0, 16:32] = fresh
-    start_rims(volume_rim, 2, (2, 3))
+    start_rims(volume_rim(0), 2, (2, 3))
     grid[1, 16:32] = swap(fresh)
-    start_rims(volume_rim, 2, (0, 1))
+    start_rims(volume_rim(0), 2, (0, 1))
     rim_send[2] = pack_rim(fresh.reshape(256, LANES), jnp.where(upper, 112, 32))
     start_rims(depth_rim, 2, (4,))
+    start_rims(volume_rim(1), 2, SIDES)
     sums_left(1)
     total[...] = jnp.zeros((2, 48, 16, LANES), F32)
     lax.fori_loop(0, VIEWS, blur_inside, 0)
@@ -543,10 +555,12 @@
     deep_rim = unpack_rim(rim_land[2], jnp.where(upper, 0, 112))
     depth_in[...] = split3(grid[0, 16:32].reshape(256, LANES) + deep_rim)
     depth_products()
-    recv_rims(volume_rim, 2, SIDES)
+    recv_rims(volume_rim(0), 2, SIDES)
+    lax.fori_loop(0, VIEWS, functools.partial(blur_rims, 0), 0)
+    recv_rims(volume_rim(1), 2, SIDES)
 
     def second(v, carry):
-        blur_rims(v, 0)
+        blur_rims(1, v, 0)
         take_ratio(v)
         return carry
 
@@ -558,10 +572,6 @@
     finish_sums(3)
     fresh = update(3)
 
-    for part in range(4):
-        packed = pack([fresh[4 * part + i] for i in range(4)])
-        for i in range(3):
-            gathered[view, 3 * part + i] = packed[i]
     size = PACKED // PIECES
 
     def half_copy(i, block):
@@ -584,31 +594,33 @@
             device_id=(at(dx, 0), tile), device_id_type=MESH,
         )
 
-    for i in range(PIECES):
-        half_copy(i, view).start()
+    for part in range(PIECES):
+        packed = pack([fresh[4 * part + i] for i in range(4)])
+        for i in range(3):
+            gathered[view, 3 * part + i] = packed[i]
+        half_copy(part, view).start()
     for dx in (1, 3, 2):
         row_copy(dx, view).start()
-    for i in range(PIECES):
-        half_copy(i, mate).wait_recv()
+
+    def unpack_out(rows, part):
+        low = unpack([gathered[2 * rows + odd, 3 * part + j] for j in range(3)])
+        high = unpack([gathered[2 * rows + 1 - odd, 3 * part + j] for j in range(3)])
+        base = pl.multiple_of(rows * CHUNK + part * 4 * Z, LANES)
+        for p in range(2):
+            for j, t in enumerate(halves_pair(low[2 * p], high[2 * p], low[2 * p + 1], high[2 * p + 1])):
+                out[:, pl.ds(base + LANES * (3 * p + j), LANES)] = t
+
+    for part in range(PIECES):
+        half_copy(part, mate).wait_recv()
         for dx in (1, 3, 2):
-            forward_copy(dx, i, mate).start()
-
-    def unpack_out(rows):
-        for part in range(4):
-            low = unpack([gathered[2 * rows + odd, 3 * part + j] for j in range(3)])
-            high = unpack([gathered[2 * rows + 1 - odd, 3 * part + j] for j in range(3)])
-            base = pl.multiple_of(rows * CHUNK + part * 4 * Z, LANES)
-            for p in range(2):
-                for j, t in enumerate(halves_pair(low[2 * p], high[2 * p], low[2 * p + 1], high[2 * p + 1])):
-                    out[:, pl.ds(base + LANES * (3 * p + j), LANES)] = t
-
-    unpack_out(cx)
+            forward_copy(dx, part, mate).start()
+        unpack_out(cx, part)
     for dx in (1, 3, 2):
-        source = at(XC - dx, 0)
-        row_copy(dx, source).wait_recv()
-        for i in range(PIECES):
-            forward_copy(dx, i, at(XC - dx, 1)).wait_recv()
-        unpack_out(source // 2)
+        row_copy(dx, at(XC - dx, 0)).wait_recv()
+    for part in range(PIECES):
+        for dx in (1, 3, 2):
+            forward_copy(dx, part, at(XC - dx, 1)).wait_recv()
+            unpack_out(at(XC - dx, 0) // 2, part)
 
     for d in (0, 1):
         when(goes[d], lambda d=d: lit_copy(d).wait_send())
@@ -621,7 +633,8 @@
         pl.when(core == c)(lambda dx=dx: tap_pass(at(XC - dx, 1)).wait_send())
     for dx in (1, 3, 2):
         tap_copy(at(dx, 0)).wait_send()
-    sent_rims(volume_rim, 2, SIDES)
+    for half in range(2):
+        sent_rims(volume_rim(half), 2, SIDES)
     sent_rims(depth_rim, 2, (4,))
     sums_left(3)
     for i in range(PIECES):
@@ -665,7 +678,7 @@
             pltpu.VMEM((256, 3 * LANES), BF16),
             vmem(VIEWS, 16, 16, LANES),
             pltpu.VMEM((256, VIEWS * 3 * LANES), BF16),
-            vmem(2, VIEWS, 16, 16, LANES),
+            vmem(VIEWS, 16, 16, LANES),
             vmem(VIEWS, 16, 16, LANES),
             vmem(2, 48, 16, LANES),
             vmem(ITERS, 4, HALF, 16, LANES),

time: 68.2 us -> 68 us (level)
  no operation moved by 1% of the time
where the time goes in v6:
time: 68 us; the launch traced here: 67.8 us
  Pallas kernels  64.9 us (95%)
  local copies, waits for them, and re-layouts  1.63 us (2%)
  between operations  1.31 us (2%)
    pallas_call x1, Pallas kernels, on_device(): pl.pallas_call(kernel, out_shape=jax.ShapeDtypeStruct((CX, YW * Z), F32),...  64.9 us
    unnamed x3, local copies, waits for them, and re-layouts  1.63 us

profile of v6, /device:TPU:32, one launch (start us, length us, event | category | flops | bytes accessed | tf_op | source)
XLA Modules:
  0.0 67.8 jit_solution(6699281526051253080)
XLA Ops:
  1.3 0.0 copy-start
  1.3 0.7 %copy-done = f32[1,31,192]{2,0,1:T(1,128)S(1)} copy-done((f32[1,31,192]{2,0,1:T(1,128)S(1)}, f32[1,31,192]{2,0,1:T(1,128)}, u32[]{:S(2)}) %copy-start) | copy-done | bytes 23832
  2.1 64.9 %shard_map.55 = f32[16,12288]{1,0:T(8,128)S(1)} custom-call(f32[16,12288]{1,0:T(8,128)} %est_hbm.1, f32[1,16,12288]{2,1,0:T(8,128)} %rec_hbm.1, f32[31,1,192]{2,1,0:T(1,128)S(1)} %bitcast.1, s32[1,1]{1,0:T(1,128)S(6)} %copy.7.lit_ref, s32[1]{0:T(128)S(6)} %copy.8.det_ref), custom_call_target="tpu_custom_call" | custom-call | tf_op jit(solution)/shard_map/pallas_call | solution.py:652
  67.0 0.9 %copy.9 = f32[16,12288]{1,0:T(8,128)} copy(f32[16,12288]{1,0:T(8,128)S(1)} %shard_map.55) | data formatting | bytes 1572864
Async XLA Ops:
  1.3 0.8 %copy-start = (f32[1,31,192]{2,0,1:T(1,128)S(1)}, f32[1,31,192]{2,0,1:T(1,128)}, u32[]{:S(2)}) copy-start(f32[1,31,192]{2,0,1:T(1,128)} %param.7) | copy-start | bytes 71428

commit v7 on v6

--- a/solution.py
+++ b/solution.py
@@ -599,7 +599,7 @@
         for i in range(3):
             gathered[view, 3 * part + i] = packed[i]
         half_copy(part, view).start()
-    for dx in (1, 3, 2):
+    for dx in (2, 1, 3):
         row_copy(dx, view).start()
 
     def unpack_out(rows, part):
@@ -612,7 +612,7 @@
 
     for part in range(PIECES):
         half_copy(part, mate).wait_recv()
-        for dx in (1, 3, 2):
+        for dx in (2, 1, 3):
             forward_copy(dx, part, mate).start()
         unpack_out(cx, part)
     for dx in (1, 3, 2):

time: 68 us -> 67.8 us (level)
  no operation moved by 1% of the time
where the time goes in v7:
time: 67.8 us; the launch traced here: 67.6 us
  Pallas kernels  64.7 us (95%)
  local copies, waits for them, and re-layouts  1.63 us (2%)
  between operations  1.31 us (2%)
    pallas_call x1, Pallas kernels, on_device(): pl.pallas_call(kernel, out_shape=jax.ShapeDtypeStruct((CX, YW * Z), F32),...  64.7 us
    unnamed x3, local copies, waits for them, and re-layouts  1.63 us

profile of v7, /device:TPU:32, one launch (start us, length us, event | category | flops | bytes accessed | tf_op | source)
XLA Modules:
  0.0 67.6 jit_solution(12497405802670095768)
XLA Ops:
  1.3 0.0 copy-start
  1.3 0.7 %copy-done = f32[1,31,192]{2,0,1:T(1,128)S(1)} copy-done((f32[1,31,192]{2,0,1:T(1,128)S(1)}, f32[1,31,192]{2,0,1:T(1,128)}, u32[]{:S(2)}) %copy-start) | copy-done | bytes 23832
  2.1 64.7 %shard_map.55 = f32[16,12288]{1,0:T(8,128)S(1)} custom-call(f32[16,12288]{1,0:T(8,128)} %est_hbm.1, f32[1,16,12288]{2,1,0:T(8,128)} %rec_hbm.1, f32[31,1,192]{2,1,0:T(1,128)S(1)} %bitcast.1, s32[1,1]{1,0:T(1,128)S(6)} %copy.7.lit_ref, s32[1]{0:T(128)S(6)} %copy.8.det_ref), custom_call_target="tpu_custom_call" | custom-call | tf_op jit(solution)/shard_map/pallas_call | solution.py:652
  66.7 0.9 %copy.9 = f32[16,12288]{1,0:T(8,128)} copy(f32[16,12288]{1,0:T(8,128)S(1)} %shard_map.55) | data formatting | bytes 1572864
Async XLA Ops:
  1.3 0.8 %copy-start = (f32[1,31,192]{2,0,1:T(1,128)S(1)}, f32[1,31,192]{2,0,1:T(1,128)}, u32[]{:S(2)}) copy-start(f32[1,31,192]{2,0,1:T(1,128)} %param.7) | copy-start | bytes 71428
